TPU v7x, 128 devices: a whole 4x4x4 slice. The times are simulated.
128 devices in a mesh: attn: 8 (over y, core), tp: 4 (over z), exp: 4 (over x).
Axes of the slice: x: 4, y: 4, z: 4, core: 2. Of those that a mesh axis runs over, the one named last changes fastest.
Arguments:
- new_query: bfloat16 [768, 3072], P(('attn', 'exp'), 'tp'), may hold values from -120 to 120
- new_kv: bfloat16 [768, 2, 512], P(('attn', 'exp'), None, 'tp'), may hold values from -4.5 to 4.5
- kv_cache: bfloat16 [768, 2, 512, 512], P(('attn', 'exp'), None, None, 'tp'), may hold values from -4.5 to 4.5
- lengths: int32 [768], P(('attn', 'exp')), may hold values from 2 to 512
- residual: bfloat16 [768, 6144], P(('attn', 'exp')), may hold values from -25 to 25
- out_proj: bfloat16 [3072, 6144], P('tp'), may hold values from -0.109375 to 0.109375
- expert_ids: int32 [768, 2], P(('attn', 'exp')), may hold values from 0 to 3, all different within a row; in each aligned block of 24 rows (0 to 23, 24 to 47, ...) at most 18 rows name the same one
- gate_weights: float32 [768, 2], P(('attn', 'exp')), may hold values from 0.1 to 1
- slot_expert: int32 [4], replicated, may hold values from 0 to 3, as said below
- moe_gain: float32 [6144], replicated, may hold values from 0.25 to 1.75
- w_gate: bfloat16 [4, 6144, 8192], P('exp', None, ('attn', 'tp')), may hold values from -0.078125 to 0.078125
- w_up: bfloat16 [4, 6144, 8192], P('exp', None, ('attn', 'tp')), may hold values from -0.078125 to 0.078125
- w_down: bfloat16 [4, 8192, 6144], P('exp', ('attn', 'tp')), may hold values from -0.125 to 0.125
Outputs:
- layer_out: bfloat16 [768, 6144], P(('attn', 'exp'), 'tp')
Inputs may be any that keep to these rules, and one draw needn't show every extreme that they name: `expert_ids`: in the rows of one device (aligned blocks of 24 requests) no expert is named more than 18 times, and that number is reached; a token's two experts differ. `slot_expert`: each expert is loaded in exactly one slot.
All inputs are finite; a program needn't handle non-finite values.
Results may differ from a plain program's by a relative error of at most 0.0059.
Values may be sent and summed in bfloat16 or wider, within the bound.
A program may use at most 128 MiB of HBM per device.

v0:
```python
import jax
import jax.numpy as jnp
from jax import lax
from jax.sharding import PartitionSpec as P

HD = 128
CAP = 18


def expert_rows(rows_in, moe_gain, w_gate, w_up, w_down):
    in_shape = rows_in.shape
    flat_rows = rows_in.reshape(-1, in_shape[-1]).astype(jnp.float32)
    spread = jnp.mean(flat_rows * flat_rows, axis=1, keepdims=True)
    normed = (flat_rows * lax.rsqrt(spread + 1e-05) * moe_gain[None, :]).astype(jnp.bfloat16)
    gate_part = jnp.dot(normed, w_gate[0], preferred_element_type=jnp.float32)
    up_part = jnp.dot(normed, w_up[0], preferred_element_type=jnp.float32)
    active = (jax.nn.silu(gate_part) * up_part).astype(jnp.bfloat16)
    result = jnp.dot(active, w_down[0], preferred_element_type=jnp.float32)
    return result.reshape(in_shape[:-1] + (result.shape[-1],))


def local(
    new_query,
    new_kv,
    kv_cache,
    lengths,
    residual,
    out_proj,
    expert_ids,
    gate_weights,
    slot_expert,
    moe_gain,
    w_gate,
    w_up,
    w_down,
):
    row_count = new_query.shape[0]
    kv_heads = new_kv.shape[2] // HD
    per_group = new_query.shape[1] // new_kv.shape[2]
    cache_span = kv_cache.shape[2]
    score_scale = HD ** (-0.5)
    queries = new_query.reshape(row_count, kv_heads, per_group, HD)
    key_rows = kv_cache[:, 0].reshape(row_count, cache_span, kv_heads, HD)
    value_rows = kv_cache[:, 1].reshape(row_count, cache_span, kv_heads, HD)
    fresh_key = new_kv[:, 0].reshape(row_count, kv_heads, HD)
    fresh_value = new_kv[:, 1].reshape(row_count, kv_heads, HD)
    scores = (
        jnp.einsum("rkgd,rckd->rkgc", queries, key_rows, preferred_element_type=jnp.float32)
        * score_scale
    )
    own_score = (
        jnp.einsum("rkgd,rkd->rkg", queries, fresh_key, preferred_element_type=jnp.float32)
        * score_scale
    )
    visible = (
        lax.broadcasted_iota(jnp.int32, (row_count, 1, 1, cache_span), 3)
        < lengths[:, None, None, None]
    )
    scores = jnp.where(visible, scores, -1e30)
    highest = jnp.maximum(jnp.max(scores, axis=3), own_score)
    weights = jnp.exp(scores - highest[..., None])
    own_weight = jnp.exp(own_score - highest)
    denominator = jnp.sum(weights, axis=3) + own_weight
    probability = (weights / denominator[..., None]).astype(jnp.bfloat16)
    own_prob = (own_weight / denominator).astype(jnp.bfloat16)
    attended_sum = jnp.einsum(
        "rkgc,rckd->rkgd", probability, value_rows, preferred_element_type=jnp.float32
    )
    attended_sum = attended_sum + jnp.einsum(
        "rkg,rkd->rkgd", own_prob, fresh_value, preferred_element_type=jnp.float32
    )
    attended = attended_sum.astype(jnp.bfloat16).reshape(row_count, -1)
    partial_value = jnp.dot(attended, out_proj, preferred_element_type=jnp.float32)
    tp_count = lax.axis_size("tp")
    attn_count = lax.axis_size("attn")
    share_width = residual.shape[1] // tp_count
    column_start = lax.axis_index("tp") * share_width
    summed = lax.psum(partial_value, "tp")
    whole_rows = residual.astype(jnp.float32) + summed
    sent_rows = whole_rows.astype(jnp.bfloat16)
    kept_cols = lax.dynamic_slice_in_dim(whole_rows, column_start, share_width, 1)
    slot_count = slot_expert.shape[0]
    chosen = expert_ids[:, :, None] == slot_expert[None, None, :]
    member = jnp.sum(chosen.astype(jnp.int32), axis=1)
    slot_weight = jnp.sum(jnp.where(chosen, gate_weights[:, :, None], 0.0), axis=1)
    position = jnp.cumsum(member, axis=0) - 1
    slot_index = lax.broadcasted_iota(jnp.int32, (1, 1, CAP), 2)
    slot_table = (position[:, :, None] == slot_index) & (member[:, :, None] > 0)
    outgoing = jnp.einsum(
        "rsc,rd->scd",
        slot_table.astype(jnp.bfloat16),
        sent_rows,
        preferred_element_type=jnp.float32,
    ).astype(jnp.bfloat16)
    incoming = lax.all_to_all(outgoing, "exp", split_axis=0, concat_axis=0, tiled=True)
    produced = expert_rows(
        lax.all_gather(
            incoming.reshape(1, slot_count * CAP, incoming.shape[2]), "attn", axis=0, tiled=True
        ),
        moe_gain,
        w_gate,
        w_up,
        w_down,
    )
    term_rows = produced.reshape(attn_count, slot_count * CAP, tp_count, share_width)
    term_rows = term_rows.transpose(0, 2, 1, 3).reshape(
        attn_count * tp_count, slot_count * CAP, share_width
    )
    combined = lax.psum_scatter(term_rows, ("attn", "tp"), scatter_dimension=0, tiled=True)
    answered = combined.reshape(slot_count, CAP, share_width).astype(jnp.bfloat16)
    returned = lax.all_to_all(answered, "exp", split_axis=0, concat_axis=0, tiled=True)
    blend_table = slot_table.astype(jnp.float32) * slot_weight[:, :, None]
    expert_mix = jnp.einsum(
        "rsc,scd->rd", blend_table, returned.astype(jnp.float32), precision=lax.Precision.HIGHEST
    )
    return (kept_cols + expert_mix).astype(jnp.bfloat16)


def solution(mesh):
    placed = (
        P(("attn", "exp"), "tp"),
        P(("attn", "exp"), None, "tp"),
        P(("attn", "exp"), None, None, "tp"),
        P(("attn", "exp")),
        P(("attn", "exp"), None),
        P("tp", None),
        P(("attn", "exp"), None),
        P(("attn", "exp"), None),
        P(),
        P(),
        P("exp", None, ("attn", "tp")),
        P("exp", None, ("attn", "tp")),
        P("exp", ("attn", "tp"), None),
    )
    return jax.shard_map(
        local, mesh=mesh, in_specs=placed, out_specs=P(("attn", "exp"), "tp"), check_vma=False
    )
```

profile of v0, /device:TPU:1, one launch (start us, length us, event | category | flops | bytes accessed | tf_op | source)
XLA Modules:
  0.0 287.9 jit_solution(15937113986498376008)
XLA Ops:
  6.5 1.0 reshape.143
  7.5 0.7 iota_compare_fusion.1
  8.3 0.8 slice_convert_fusion
  9.1 0.1 fusion.51
  9.2 2.9 %fusion.58 = (f32[24,6]{1,0:T(8,128)S(1)}, f32[24,6,512]{2,1,0:T(8,128)S(1)}) fusion(bf16[24,6,128]{2,1,0:T(8,128)(2,1)S(1)} %reshape.143, bf16[24,2,512,128]{3,2,1,0:T(8,128)(2,1)} %param.15, pred[24,512]{1,0:T(8,128)(4,1)S(1)} %iota_compare_fusion.1), kind=kOutput, calls=%fused_computation.63 | convolution fusion | flops 19095408 | bytes 3490368 | tf_op jit(solution)/shard_map/rkgd,rckd->rkgc/dot_general | solution.py:48
  12.1 0.2 fusion.33
  12.4 2.5 fusion.30
  14.9 5.9 %fusion.42 = f32[24,6144]{1,0:T(8,128)} fusion(bf16[768,6144]{1,0:T(8,128)(2,1)} %param.18, bf16[3,8,6,128]{3,2,1,0:T(8,128)(2,1)S(1)} %bitcast.79), kind=kOutput, calls=%fused_computation.37 | convolution fusion | flops 226492416 | bytes 10063872 | tf_op jit(solution)/shard_map/dot_general | solution.py:73
  20.9 0.1 copy.43
  21.1 0.1 copy.44
  21.2 44.8 %all-reduce.2.cloned.1.call-done = f32[24,6144]{1,0:T(8,128)} async-done(((f32[24,6144]{1,0:T(8,128)}), f32[24,6144]{1,0:T(8,128)}) %all-reduce.2.cloned.1.call-update) | async-done | bytes 589840 | tf_op jit(solution)/shard_map/psum | solution.py:78
  66.0 1.1 convert_add_fusion
  67.1 0.8 copy-done.4
  67.9 0.6 convolution_convert_fusion
  68.5 17.4 %all_to_all.10 = bf16[4,18,6144]{2,1,0:T(8,128)(2,1)} all-to-all(bf16[4,18,6144]{2,1,0:T(8,128)(2,1)S(1)} %convolution_convert_fusion), channel_id=1, replica_groups=mesh['attn'=8,'tp'=4,'exp'=4] {'exp'}, dimensions={0} | all-to-all | bytes 1769472 | tf_op jit(solution)/shard_map/all_to_all | solution.py:95
  85.8 2.5 reshape.149
  88.4 0.2 reduce-scatter.2.cloned.1.call-start
  88.6 4.6 %copy.51 = bf16[6144,256]{1,0:T(8,128)(2,1)} copy(bf16[6144,256]{0,1:T(8,128)(2,1)} %bitcast.77) | data formatting | bytes 6291456 | tf_op jit(solution)/shard_map/dot_general | solution.py:18
  93.3 41.6 %all-gather.2.cloned.1.call-done = bf16[8,72,6144]{2,1,0:T(8,128)(2,1)} async-done(((bf16[1,72,6144]{2,1,0:T(8,128)(2,1)}), bf16[8,72,6144]{2,1,0:T(8,128)(2,1)}) %all-gather.2.cloned.1.call-update) | async-done | bytes 7077904 | tf_op jit(solution)/shard_map/all_gather | solution.py:97
  134.9 4.6 %fusion = f32[8,72]{1,0:T(8,128)S(1)} fusion(bf16[8,72,6144]{2,1,0:T(8,128)(2,1)} %all-gather.2.cloned.1.call-done), kind=kLoop, calls=%fused_computation.2 | loop fusion | flops 10616256 | bytes 7080192 | tf_op jit(solution)/shard_map/reduce_sum | solution.py:13
  139.6 0.4 copy-done.1
  139.9 5.5 %fusion.2 = bf16[8,72,6144]{2,1,0:T(8,128)(2,1)} fusion(bf16[8,72,6144]{2,1,0:T(8,128)(2,1)S(1)} %copy-done.1, f32[6144]{0:T(1024)S(1)} %copy-done.6, f32[8,72]{1,0:T(8,128)S(1)} %add_rsqrt_fusion), kind=kLoop, calls=%fused_computation.4 | loop fusion | flops 14155776 | bytes 14182656 | tf_op jit(solution)/shard_map/convert_element_type | solution.py:14
  145.4 5.1 %fusion.9 = f32[576,256]{1,0:T(8,128)S(1)} fusion(bf16[576,6144]{1,0:T(8,128)(2,1)} %bitcast.75, bf16[1,6144,256]{2,1,0:T(8,128)(2,1)S(1)} %copy-done), kind=kOutput, calls=%fused_computation.12 | convolution fusion | flops 1811939328 | bytes 10813440 | tf_op jit(solution)/shard_map/dot_general | solution.py:15
  150.6 0.7 copy-done.10
  151.4 2.0 fusion.18
  153.4 7.1 %fusion.59 = f32[8,72,4,1536]{3,1,2,0:T(8,128)} fusion(bf16[8,72,256,1]{2,1,3,0:T(8,128)(2,1)S(1)} %bitcast.78, bf16[4,1536,256,1]{2,1,0,3:T(8,128)(2,1)S(1)} %bitcast.74), kind=kOutput, calls=%fused_computation.64 | convolution fusion | flops 1811939328 | bytes 17596416 | tf_op jit(solution)/shard_map/dot_general | solution.py:18
  160.5 107.3 %reduce-scatter.2.cloned.1.call-done = f32[1,72,1536]{2,1,0:T(8,128)} async-done(((f32[32,72,1536]{2,1,0:T(8,128)}), f32[1,72,1536]{2,1,0:T(8,128)}) %reduce-scatter.2.cloned.1.call-update) | async-done | bytes 442384 | tf_op jit(solution)/shard_map/reduce_scatter | solution.py:109
  267.8 1.0 convert_element_type.63
  268.9 0.8 convert_element_type.64
  269.7 4.0 %all-to-all-start.1 = ((bf16[4,18,1536]{2,1,0:T(8,128)(2,1)}), bf16[4,18,1536]{2,1,0:T(8,128)(2,1)S(1)}, u32[]{:S(2)}, u32[]{:S(2)}) async-start(bf16[4,18,1536]{2,1,0:T(8,128)(2,1)} %convert_element_type.64), calls=%async_computation.2 | async-start | bytes 589824 | tf_op jit(solution)/shard_map/all_to_all | solution.py:111
  273.7 5.6 %all-to-all-done.1 = bf16[4,18,1536]{2,1,0:T(8,128)(2,1)S(1)} async-done(((bf16[4,18,1536]{2,1,0:T(8,128)(2,1)}), bf16[4,18,1536]{2,1,0:T(8,128)(2,1)S(1)}, u32[]{:S(2)}, u32[]{:S(2)}) %all-to-all-start.1) | async-done | bytes 221216 | tf_op jit(solution)/shard_map/all_to_all | solution.py:111
  279.3 2.0 fusion.14
  (33 shorter events, 0.4 us)
Async XLA Ops:
  6.5 138.9 %copy-start = (bf16[1,6144,256]{2,1,0:T(8,128)(2,1)S(1)}, bf16[1,6144,256]{2,1,0:T(8,128)(2,1)}, u32[]{:S(2)}) copy-start(bf16[1,6144,256]{2,1,0:T(8,128)(2,1)} %param.23) | copy-start | bytes 9437188
  6.5 59.4 %all-reduce.2.cloned.1.call-start = ((), (), s32[]{:S(2)}) async-start(), calls=%async_computation.3 | async-start | bytes 1179648 | tf_op jit(solution)/shard_map/psum | solution.py:78
  14.9 6.0 %copy-start.7 = (s32[24,2]{0,1:T(2,128)S(1)}, s32[24,2]{0,1:T(2,128)}, u32[]{:S(2)}) copy-start(s32[24,2]{0,1:T(2,128)} %param.19) | copy-start | bytes 580
  14.9 6.0 %copy-start.8 = (s32[4]{0:T(128)S(1)}, s32[4]{0:T(128)}, u32[]{:S(2)}) copy-start(s32[4]{0:T(128)} %param.21) | copy-start | bytes 52
  14.9 51.1 %copy-start.5 = (bf16[24,6144]{1,0:T(8,128)(2,1)S(1)}, bf16[24,6144]{1,0:T(8,128)(2,1)}, u32[]{:S(2)}) copy-start(bf16[24,6144]{1,0:T(8,128)(2,1)} %param.17) | copy-start | bytes 884740
  20.8 114.1 %all-gather.2.cloned.1.call-start = ((), (), s32[]{:S(2)}) async-start(), calls=%async_computation.4 | async-start | bytes 7962624 | tf_op jit(solution)/shard_map/all_gather | solution.py:97
  67.1 0.8 copy-start.4
  88.4 179.5 %reduce-scatter.2.cloned.1.call-start = ((), (), s32[]{:S(2)}) async-start(), calls=%async_computation.5 | async-start | bytes 14598144 | tf_op jit(solution)/shard_map/reduce_scatter | solution.py:109
  88.6 50.9 %copy-start.6 = (f32[6144]{0:T(1024)S(1)}, f32[6144]{0:T(1024)}, u32[]{:S(2)}) copy-start(f32[6144]{0:T(1024)} %param.22) | copy-start | bytes 73732
  134.9 5.0 %copy-start.1 = (bf16[8,72,6144]{2,1,0:T(8,128)(2,1)S(1)}, bf16[8,72,6144]{2,1,0:T(8,128)(2,1)}, u32[]{:S(2)}) copy-start(bf16[8,72,6144]{2,1,0:T(8,128)(2,1)} %all-gather.2.cloned.1.call-done) | copy-start | bytes 21233668
  145.4 5.2 %copy-start.3 = (bf16[8,72,6144]{2,1,0:T(8,128)(2,1)S(1)}, bf16[8,72,6144]{2,1,0:T(8,128)(2,1)}, u32[]{:S(2)}) copy-start(bf16[8,72,6144]{2,1,0:T(8,128)(2,1)} %fusion.2) | copy-start | bytes 21233668
  145.4 5.9 %copy-start.10 = (bf16[1,6144,256]{2,1,0:T(8,128)(2,1)S(1)}, bf16[1,6144,256]{2,1,0:T(8,128)(2,1)}, u32[]{:S(2)}) copy-start(bf16[1,6144,256]{2,1,0:T(8,128)(2,1)} %param.24) | copy-start | bytes 9437188
  151.4 2.0 copy-start.2
  160.5 113.1 %copy-start.9 = (f32[24,2]{0,1:T(2,128)S(1)}, f32[24,2]{0,1:T(2,128)}, u32[]{:S(2)}) copy-start(f32[24,2]{0,1:T(2,128)} %param.20) | copy-start | bytes 580
  269.7 9.7 %all-to-all-start.1 = ((bf16[4,18,1536]{2,1,0:T(8,128)(2,1)}), bf16[4,18,1536]{2,1,0:T(8,128)(2,1)S(1)}, u32[]{:S(2)}, u32[]{:S(2)}) async-start(bf16[4,18,1536]{2,1,0:T(8,128)(2,1)} %convert_element_type.64), calls=%async_computation.2 | async-start | bytes 589824 | tf_op jit(solution)/shard_map/all_to_all | solution.py:111
Sparse Core Ops, SparseCore 0:
  20.9 45.0 all-reduce.1
  88.5 46.3 all-gather.1
  160.6 107.1 reduce-scatter.1
where the time goes:
time: 290 us; the launch traced here: 288 us
  waiting for transfers between devices  199 us (69%)
  matrix products  28.3 us (10%)
  blocking collectives  17.4 us (6%)
  other arithmetic  14.3 us (5%)
  between operations  13.3 us (5%)
  local copies, waits for them, and re-layouts  11 us (4%)
  starting transfers between devices  4.23 us (1%)
    reduce_scatter x1, waiting for transfers between devices, local(): lax.psum_scatter(term_rows, ('attn', 'tp'), scatter_dimension=0, tiled=True)  107 us
    psum x1, waiting for transfers between devices, local(): summed = lax.psum(partial_value, 'tp')  44.8 us
    all_gather x1, waiting for transfers between devices, local(): lax.all_gather(incoming.reshape(1, slot_count * CAP, incoming.shape[2]),...  41.6 us
    all_to_all x1, blocking collectives, local(): lax.all_to_all(outgoing, 'exp', split_axis=0, concat_axis=0, tiled=True)  17.4 us
    dot_general x1, matrix products, expert_rows(): result = jnp.dot(active, w_down[0], preferred_element_type=jnp.float32)  7.12 us
    dot_general x1, matrix products, local(): jnp.dot(attended, out_proj, preferred_element_type=jnp.float32)  5.88 us
  transfers between devices with their start and end apart: 4, of which 4 were waited for; matrix products, arithmetic and copies ran while one was open for 2% of the time, Pallas kernels for 0%

commit v1 on v0

v1 whole, which is shorter than its diff:
```python
import jax
import jax.numpy as jnp
from jax import lax
from jax.experimental import pallas as pl
from jax.experimental.pallas import tpu as pltpu
from jax.sharding import PartitionSpec as P

MESH = pl.DeviceIdType.MESH
F32 = jnp.float32
BF16 = jnp.bfloat16

HD = 128
HEADS = 6
R = 24
R2 = 48
CACHE = 512
D = 6144
QD = 1536
W = 256
SEMS = 288

STREAMS = (("x", "y", "z"), ("y", "z", "x"), ("z", "x", "y"))
FORWARD_UP = (0, 3)
FORWARD_DOWN = (1, 2)


def wrap(v):
    return lax.rem(v + 4, 4)


def kernel(
    lengths, slot_expert, query, new_kv, residual, ids, gate_w, gain, cache, out_proj, w_gate, w_up, w_down,
    out,
    k_buf, v_buf, op_buf, wg, wu, wd, q_pad, kn, vn, scores, attn_out,
    info, res_send, res_recv, z_send, z_recv, hidden,
    x_all, ssum, acc_g, acc_u, act,
    sib_out, sib_in, part, d2_in, plane_in, row_out, row_in, row_own, blk_out, blk_in, fin_send, fin,
    send_sems, recv_sems, local_sems,
):
    attn = lax.axis_index("attn")
    me = {"y": attn // 2, "c": lax.rem(attn, 2), "z": lax.axis_index("tp"), "x": lax.axis_index("exp")}
    c, other = me["c"], 1 - me["c"]

    def device(c=None, **steps):
        at = dict(me)
        for axis, step in steps.items():
            at[axis] = wrap(at[axis] + step)
        if c is not None:
            at["c"] = c
        return (at["y"] * 2 + at["c"], at["z"], at["x"])

    sibling = device(c=other)

    def local(src, dst, i):
        return pltpu.make_async_copy(src, dst, local_sems.at[i])

    k_copies = [local(cache.at[pl.ds(i * 6, 6), 0], k_buf.at[pl.ds(i * 6, 6)], i) for i in range(4)]
    v_copies = [local(cache.at[pl.ds(i * 6, 6), 1], v_buf.at[pl.ds(i * 6, 6)], 4 + i) for i in range(4)]
    op_copies = {
        j: local(out_proj.at[:, pl.ds(pl.multiple_of(wrap(me["z"] + j) * QD, QD), QD)], op_buf.at[j], 8 + j)
        for j in (2, 1, 3, 0)
    }
    w_copies = [local(w_gate.at[0], wg, 12), local(w_up.at[0], wu, 13)]
    wd_copies = []
    for half, h in ((0, c), (1, other)):
        for z in range(4):
            for s in range(3):
                start = pl.multiple_of(z * QD + s * 512 + h * W, W)
                wd_copies.append(
                    local(w_down.at[0, :, pl.ds(start, W)], wd.at[half, z, s], 14 + half * 12 + z * 3 + s)
                )
    for cp in k_copies + v_copies:
        cp.start()
    for j in (2, 1, 3, 0):
        op_copies[j].start()

    barrier = pltpu.get_barrier_semaphore()
    partners = [device(c=k, z=j) for j in (1, 2, 3) for k in (0, 1)] + [sibling]
    partners += [device(**{a: j}) for a in ("x", "y") for j in (1, 2, 3)]
    for p in partners:
        pl.semaphore_signal(barrier, inc=1, device_id=p, device_id_type=MESH)

    table = {}
    started = []

    def sem(key):
        if key not in table:
            table[key] = len(table)
            assert len(table) <= SEMS
        return table[key]

    def send(src, dst, key, to, index=None):
        i = sem(key)
        cp = pltpu.make_async_remote_copy(
            src_ref=src, dst_ref=dst, send_sem=send_sems.at[i],
            recv_sem=recv_sems.at[i if index is None else index],
            device_id=to, device_id_type=MESH,
        )
        cp.start()
        started.append(cp)

    def arrived(dst, key, index=None):
        i = sem(key) if index is None else index
        pltpu.make_async_remote_copy(
            src_ref=dst, dst_ref=dst, send_sem=send_sems.at[i], recv_sem=recv_sems.at[i],
            device_id=sibling, device_id_type=MESH,
        ).wait_recv()

    def drain():
        for cp in started:
            cp.wait_send()
        started.clear()

    z_sem = {}
    for j in range(4):
        z_sem[j] = sem(("zr", j, 0))
        sem(("zr", j, 1))

    lane = lax.broadcasted_iota(jnp.int32, (R, 128), 1)
    mine = jnp.zeros((R, 128), F32)
    for s in range(4):
        hit = jnp.where(ids[...] == slot_expert[s], gate_w[...], 0.0)
        mine = mine + jnp.where(lane == s, jnp.sum(hit, axis=1, keepdims=True), 0.0)
    info[c, me["y"], me["x"]] = mine

    def res_part(h):
        return jnp.concatenate(
            [residual[:, pl.ds(pl.multiple_of(me["z"] * QD + s * 512 + h * W, W), W)] for s in range(3)], axis=1
        ).astype(F32)

    res_send[...] = res_part(other)

    pl.semaphore_wait(barrier, len(partners))
    for j in (1, 3, 2):
        spot = info.at[c, me["y"], me["x"]]
        send(spot, spot, ("info x", j), device(x=j))
    send(res_send, res_recv, ("res",), sibling)

    for h in range(8):
        if h < HEADS:
            q_pad[pl.ds(h, R, stride=8), :] = query[:, h * HD : (h + 1) * HD].astype(F32)
        else:
            q_pad[pl.ds(h, R, stride=8), :] = jnp.zeros((R, HD), F32)
        kn[pl.ds(h, R, stride=8), :] = new_kv[:, :HD].astype(F32)
        vn[pl.ds(h, R, stride=8), :] = new_kv[:, HD:].astype(F32)
    scale = HD ** (-0.5)
    position = lax.broadcasted_iota(jnp.int32, (8, CACHE), 1)

    for i in range(4):
        k_copies[i].wait()
        for r in range(i * 6, i * 6 + 6):
            s = lax.dot_general(
                q_pad[r * 8 : r * 8 + 8, :].astype(BF16), k_buf[r], (((1,), (1,)), ((), ())),
                preferred_element_type=F32,
            ) * scale
            scores[r * 8 : r * 8 + 8, :] = jnp.where(position < lengths[r], s, -1e30)
    own_score = jnp.sum(q_pad[...] * kn[...], axis=1, keepdims=True) * scale
    raw = scores[...]
    top = jnp.maximum(jnp.max(raw, axis=1, keepdims=True), own_score)
    weight = jnp.exp(raw - top)
    own_weight = jnp.exp(own_score - top)
    total = jnp.sum(weight, axis=1, keepdims=True) + own_weight
    scores[...] = weight / total
    own_prob = (own_weight / total).astype(BF16).astype(F32)
    for i in range(4):
        v_copies[i].wait()
        for r in range(i * 6, i * 6 + 6):
            attn_out[r * 8 : r * 8 + 8, :] = jnp.dot(
                scores[r * 8 : r * 8 + 8, :].astype(BF16), v_buf[r], preferred_element_type=F32
            )
    attn_out[...] = attn_out[...] + own_prob * vn[...]
    attended = jnp.concatenate([attn_out[pl.ds(h, R, stride=8), :] for h in range(HEADS)], axis=1).astype(BF16)

    for cp in w_copies + wd_copies:
        cp.start()

    def pack(v):
        return jnp.concatenate([v[:, :384], v[:, 384:]], axis=0).astype(BF16)

    def unpack(v):
        v = v.astype(F32)
        return jnp.concatenate([v[:R], v[R:]], axis=1)

    own_term = None
    for j in (2, 1, 3, 0):
        op_copies[j].wait()
        term = jnp.dot(attended, op_buf[j], preferred_element_type=F32)
        halves = [
            jnp.concatenate([term[:, s * 512 + h * W : s * 512 + (h + 1) * W] for s in range(3)], axis=1)
            for h in range(2)
        ]
        if j:
            for h in range(2):
                z_send[j, h] = pack(halves[h])
                send(z_send.at[j, h], z_recv.at[j, c], ("zs", j, h), device(c=h, z=j), z_sem[j] + c)
        else:
            hidden[0] = halves[0]
            hidden[1] = halves[1]
            own_term = hidden[c]
            z_send[0, 0] = pack(hidden[other])
            send(z_send.at[0, 0], z_recv.at[0, c], ("zs", 0, 0), sibling, z_sem[0] + c)

    for j in (1, 3, 2):
        arrived(info.at[c, me["y"], wrap(me["x"] - j)], ("info x", j))
    for j in (1, 3, 2):
        spot = info.at[c, me["y"]]
        send(spot, spot, ("info y", j), device(y=j))

    acc_g[...] = jnp.zeros_like(acc_g)
    acc_u[...] = jnp.zeros_like(acc_u)
    ssum[...] = jnp.zeros_like(ssum)

    arrived(res_recv, ("res",))
    mine = own_term + res_part(c)
    theirs = res_recv[...]
    arrived(z_recv.at[0, other], None, z_sem[0] + other)
    theirs = theirs + unpack(z_recv[0, other])
    for j in (1, 3, 2):
        for k in range(2):
            arrived(z_recv.at[j, k], None, z_sem[j] + k)
        mine = mine + unpack(z_recv[j, c])
        theirs = theirs + unpack(z_recv[j, other])
    hidden[c] = mine
    hidden[other] = theirs
    sent = jnp.concatenate([hidden[0], hidden[1]], axis=0).astype(BF16)

    place = [tuple(me[a] for a in axes) for axes in STREAMS]
    for s, (a1, a2, a3) in enumerate(STREAMS):
        p1, p2, p3 = place[s]
        x_all[c, s, p3, p2, p1] = sent[:, s * W : (s + 1) * W]
    for s, (a1, a2, a3) in enumerate(STREAMS):
        p1, p2, p3 = place[s]
        for j in (1, 3, 2):
            spot = x_all.at[c, s, p3, p2, p1]
            send(spot, spot, ("g1", s, j), device(**{a1: j}))

    def row(s, j3, j2, core):
        _, p2, p3 = place[s]
        return x_all.at[core, s, wrap(p3 + j3), wrap(p2 + j2)]

    def share(s, j3, j2):
        spot = row(s, j3, j2, c)
        send(spot, spot, ("gs", s, j3, j2), sibling)

    def out3(s, j2):
        a3 = STREAMS[s][2]
        spot = row(s, 0, j2, c)
        for j in (1, 3):
            send(spot, spot, ("g3", s, j, j2), device(**{a3: j}))
        share(s, 0, j2)

    for s, (a1, a2, a3) in enumerate(STREAMS):
        p1, p2, p3 = place[s]
        for j in (1, 3, 2):
            arrived(x_all.at[c, s, p3, p2, wrap(p1 - j)], ("g1", s, j))
        spot = row(s, 0, 0, c)
        for j in (1, 3, 2):
            send(spot, spot, ("g2", s, j), device(**{a2: j}))
        out3(s, 0)

    def take2(j):
        for s in range(3):
            arrived(row(s, 0, -j, c), ("g2", s, j))
            out3(s, 4 - j)

    def take3(j2):
        for s in range(3):
            a3 = STREAMS[s][2]
            for j in (1, 3):
                spot = row(s, -j, j2, c)
                arrived(spot, ("g3", s, j, j2))
                if j2 in (FORWARD_UP if j == 1 else FORWARD_DOWN):
                    send(spot, spot, ("g4", s, j2), device(**{a3: j}))
                share(s, 4 - j, j2)

    def take4(j2):
        for s in range(3):
            spot = row(s, 2, j2, c)
            arrived(spot, ("g4", s, j2))
            share(s, 2, j2)

    def shared(s, j3):
        for j2 in range(4):
            arrived(row(s, j3, j2, other), ("gs", s, j3, j2))

    def multiply(s, j3):
        q = wrap(place[s][2] + j3)

        def step(i, carry):
            z = q if s == 0 else i
            spot = (i,) if s == 0 else ((slice(None), q) if s == 1 else (q,))
            g = u = sq = None
            for h in range(2):
                if s == 2:
                    x = x_all[h, s, q, :, i]
                else:
                    x = x_all[h, s, q, i]
                x = x.reshape(4 * R2, W).astype(F32)
                k = z * 6 + s * 2 + h
                part_sq = x * x
                part_sq = part_sq[:, :128] + part_sq[:, 128:]
                xb = (x * gain[k]).astype(BF16)
                rows = pl.ds(pl.multiple_of(k * W, W), W)
                part_g = jnp.dot(xb, wg[rows, :], preferred_element_type=F32)
                part_u = jnp.dot(xb, wu[rows, :], preferred_element_type=F32)
                g = part_g if g is None else g + part_g
                u = part_u if u is None else u + part_u
                sq = part_sq if sq is None else sq + part_sq
            acc_g[spot] = acc_g[spot] + g.reshape(4, R2, W)
            acc_u[spot] = acc_u[spot] + u.reshape(4, R2, W)
            ssum[spot] = ssum[spot] + sq.reshape(4, R2, 128)
            return carry

        lax.fori_loop(0, 4, step, 0)

    take2(1)
    take3(0)
    take2(3)
    take3(3)
    take2(2)
    for j in (1, 3, 2):
        arrived(info.at[c, wrap(me["y"] - j)], ("info y", j))
    send(info.at[c], info.at[c], ("info c",), sibling)
    for cp in w_copies + wd_copies:
        cp.wait()
    for s in range(3):
        shared(s, 0)
        multiply(s, 0)
    take3(1)
    take3(2)
    take4(0)
    for s in range(3):
        for j3 in (1, 3):
            shared(s, j3)
            multiply(s, j3)
    take4(3)
    take4(1)
    take4(2)
    arrived(info.at[other], ("info c",))
    for s in range(3):
        shared(s, 2)
        multiply(s, 2)

    lane4 = lax.broadcasted_iota(jnp.int32, (4, R2, 128), 2)

    def activate(i, carry):
        both = jnp.concatenate([info[0, i], info[1, i]], axis=1)
        chosen = jnp.sum(jnp.where(lane4 == me["x"], both, 0.0), axis=2, keepdims=True)
        inv = lax.rsqrt(jnp.sum(ssum[i], axis=2, keepdims=True) / D + 1e-05)
        g = acc_g[i] * inv
        u = acc_u[i] * inv
        act[i] = (g / (1.0 + jnp.exp(-g)) * u * chosen).astype(BF16)
        return carry

    lax.fori_loop(0, 4, activate, 0)

    def down(s, j3, half, store):
        q = wrap(place[s][2] + j3)

        def step(i, carry):
            if s == 0:
                a, w = act[i], wd[half, q, s]
            elif s == 1:
                a, w = act[:, q], wd[half, i, s]
            else:
                a, w = act[q], wd[half, i, s]
            y = jnp.dot(a.reshape(4 * R2, W), w, preferred_element_type=F32).reshape(4, R2, W)
            store(y, (slice(None), i) if s == 2 else (i,))
            return carry

        lax.fori_loop(0, 4, step, 0)

    def for_sibling(s, j3):
        def store(y, spot):
            sib_out[(s, j3) + spot] = y.astype(BF16)

        down(s, j3, 1, store)
        send(sib_out.at[s, j3], sib_in.at[s, j3], ("rs", s, j3), sibling)

    def for_chip(s, j3):
        arrived(sib_in.at[s, j3], ("rs", s, j3))

        def store(y, spot):
            part[(s, j3) + spot] = (y + sib_in[(s, j3) + spot].astype(F32)).astype(BF16)

        down(s, j3, 0, store)

    def second(s, j2):
        return wrap(place[s][1] + j2)

    def send_far(s):
        a3 = STREAMS[s][2]
        for j, rows in ((1, FORWARD_UP), (3, FORWARD_DOWN)):
            for j2 in rows:
                r = second(s, j2)
                send(part.at[s, 2, r], d2_in.at[s, r], ("r4", s, j2), device(**{a3: j}))

    def send_near(s, j, j2):
        r = second(s, j2)
        send(part.at[s, j, r], plane_in.at[s, j // 2, r], ("r3", s, j, j2), device(**{STREAMS[s][2]: j}))

    for s in range(3):
        for_sibling(s, 2)
    for s in range(3):
        for_sibling(s, 1)
        for_chip(s, 2)
        send_far(s)
    for s in range(3):
        for_sibling(s, 3)
        for_chip(s, 1)
        for j2 in FORWARD_DOWN:
            send_near(s, 1, j2)
    for s in range(3):
        for_sibling(s, 0)
        for_chip(s, 3)
        for j2 in FORWARD_UP:
            send_near(s, 3, j2)
    for s in range(3):
        for_chip(s, 0)
    drain()
    for j2 in (2, 3, 1, 0):
        j = 1 if j2 in FORWARD_UP else 3
        for s in range(3):
            r = second(s, j2)
            arrived(d2_in.at[s, r], ("r4", s, j2))
            part[s, j, r] = (part[s, j, r].astype(F32) + d2_in[s, r].astype(F32)).astype(BF16)
            send_near(s, j, j2)

    for j2 in (2, 3, 1, 0):
        for s in range(3):
            r = second(s, j2)
            for j in (1, 3):
                arrived(plane_in.at[s, j // 2, r], ("r3", s, j, j2))
            v = part[s, 0, r].astype(F32) + plane_in[s, 0, r].astype(F32) + plane_in[s, 1, r].astype(F32)
            if j2:
                row_out[s, j2 - 1] = v.astype(BF16)
                send(row_out.at[s, j2 - 1], row_in.at[s, j2 - 1], ("r2", s, j2), device(**{STREAMS[s][1]: j2}))
            else:
                row_own[s] = v
    for s in range(3):
        v = row_own[s]
        for j2 in (1, 2, 3):
            arrived(row_in.at[s, j2 - 1], ("r2", s, j2))
            v = v + row_in[s, j2 - 1].astype(F32)
        row_own[s] = v
        for j1 in (2, 1, 3):
            blk_out[s, j1 - 1] = row_own[s, wrap(place[s][0] + j1)].astype(BF16)
            send(blk_out.at[s, j1 - 1], blk_in.at[s, j1 - 1], ("r1", s, j1), device(**{STREAMS[s][0]: j1}))
    for s in range(3):
        v = row_own[s, place[s][0]]
        for j1 in (1, 2, 3):
            arrived(blk_in.at[s, j1 - 1], ("r1", s, j1))
            v = v + blk_in[s, j1 - 1].astype(F32)
        for k in range(2):
            hidden[k, :, s * W : (s + 1) * W] = hidden[k, :, s * W : (s + 1) * W] + v[k * R : (k + 1) * R]
    fin_send[...] = hidden[other]
    send(fin_send, fin.at[c], ("fin",), sibling)
    fin[c] = hidden[c]
    drain()
    arrived(fin.at[other], ("fin",))
    for s in range(3):
        for h in range(2):
            out[:, s * 512 + h * W : s * 512 + (h + 1) * W] = fin[h, :, s * W : (s + 1) * W].astype(BF16)


def local_step(
    new_query, new_kv, kv_cache, lengths, residual, out_proj, expert_ids, gate_weights, slot_expert, moe_gain,
    w_gate, w_up, w_down,
):
    vmem = pl.BlockSpec(memory_space=pltpu.VMEM)
    smem = pl.BlockSpec(memory_space=pltpu.SMEM)
    anywhere = pl.BlockSpec(memory_space=pl.ANY)
    v = pltpu.VMEM
    return pl.pallas_call(
        kernel,
        out_shape=jax.ShapeDtypeStruct((R, QD), BF16),
        in_specs=[smem, smem] + [vmem] * 6 + [anywhere] * 5,
        out_specs=vmem,
        scratch_shapes=[
            v((R, CACHE, HD), BF16),
            v((R, CACHE, HD), BF16),
            v((4, HEADS * HD, QD), BF16),
            v((D, W), BF16),
            v((D, W), BF16),
            v((2, 4, 3, W, W), BF16),
            v((R * 8, HD), F32),
            v((R * 8, HD), F32),
            v((R * 8, HD), F32),
            v((R * 8, CACHE), F32),
            v((R * 8, HD), F32),
            v((2, 4, 4, R, 128), F32),
            v((R, 3 * W), F32),
            v((R, 3 * W), F32),
            v((4, 2, R2, 384), BF16),
            v((4, 2, R2, 384), BF16),
            v((2, R, 3 * W), F32),
            v((2, 3, 4, 4, 4, R2, W), BF16),
            v((4, 4, R2, 128), F32),
            v((4, 4, R2, W), F32),
            v((4, 4, R2, W), F32),
            v((4, 4, R2, W), BF16),
            v((3, 4, 4, 4, R2, W), BF16),
            v((3, 4, 4, 4, R2, W), BF16),
            v((3, 4, 4, 4, R2, W), BF16),
            v((3, 4, 4, R2, W), BF16),
            v((3, 2, 4, 4, R2, W), BF16),
            v((3, 3, 4, R2, W), BF16),
            v((3, 3, 4, R2, W), BF16),
            v((3, 4, R2, W), F32),
            v((3, 3, R2, W), BF16),
            v((3, 3, R2, W), BF16),
            v((R, 3 * W), F32),
            v((2, R, 3 * W), F32),
            pltpu.SemaphoreType.DMA((SEMS,)),
            pltpu.SemaphoreType.DMA((SEMS,)),
            pltpu.SemaphoreType.DMA((38,)),
        ],
        compiler_params=pltpu.CompilerParams(
            collective_id=0, has_side_effects=True, vmem_limit_bytes=62 * 2**20
        ),
        name="decode_layer",
    )(
        lengths, slot_expert, new_query, new_kv.reshape(R, 2 * HD), residual, expert_ids, gate_weights,
        moe_gain.reshape(D // W, 1, W), kv_cache, out_proj, w_gate, w_up, w_down,
    )


def solution(mesh):
    placed = (
        P(("attn", "exp"), "tp"),
        P(("attn", "exp"), None, "tp"),
        P(("attn", "exp"), None, None, "tp"),
        P(("attn", "exp")),
        P(("attn", "exp"), None),
        P("tp", None),
        P(("attn", "exp"), None),
        P(("attn", "exp"), None),
        P(),
        P(),
        P("exp", None, ("attn", "tp")),
        P("exp", None, ("attn", "tp")),
        P("exp", ("attn", "tp"), None),
    )
    return jax.shard_map(
        local_step, mesh=mesh, in_specs=placed, out_specs=P(("attn", "exp"), "tp"), check_vma=False
    )
```

time: 290 us -> 105 us (0.36)
  waiting for transfers between devices: 199 us -> 0 us
  Pallas kernels: 0 us -> 98.7 us
  matrix products: 28.3 us -> 0 us
  blocking collectives: 17.4 us -> 0 us
  other arithmetic: 14.3 us -> 0 us
  between operations: 13.3 us -> 0.01 us
  local copies, waits for them, and re-layouts: 11 us -> 5.54 us
  starting transfers between devices: 4.23 us -> 0 us
    reduce_scatter x1 -> x0, waiting for transfers between devices: 107 us -> none  [local(): lax.psum_scatter(term_rows, ('attn', 'tp'), scatter_dimension=0, tiled=True)]
    pallas_call x0 -> x1, Pallas kernels: none -> 98.7 us  [local_step(): pl.pallas_call(kernel, out_shape=jax.ShapeDtypeStruct((R, QD), BF16), in_...]
    psum x1 -> x0, waiting for transfers between devices: 44.8 us -> none  [local(): summed = lax.psum(partial_value, 'tp')]
    all_gather x1 -> x0, waiting for transfers between devices: 41.6 us -> none  [local(): lax.all_gather(incoming.reshape(1, slot_count * CAP, incoming.shape[2]),...]
    dot_general x9 -> x0, matrix products: 28.3 us -> none  [the longest x1 7.12 us: expert_rows(): result = jnp.dot(active, w_down[0], preferred_element_type=jnp.float32)]
    all_to_all x1 -> x0, blocking collectives: 17.4 us -> none  [local(): lax.all_to_all(outgoing, 'exp', split_axis=0, concat_axis=0, tiled=True)]
    convert_element_type x2 -> x0, other arithmetic: 6.54 us -> none  [the longest x1 5.5 us: expert_rows(): (flat_rows * lax.rsqrt(spread + 1e-05) * moe_gain[None, :]).astype(jnp.bf...]
    all_to_all x1 -> x0, waiting for transfers between devices: 5.62 us -> none  [local(): lax.all_to_all(answered, 'exp', split_axis=0, concat_axis=0, tiled=True)]
  transfers between devices with their start and end apart: 4 -> 0, of which waited for: 4 -> 0; matrix products, arithmetic and copies ran while one was open for 2% -> 0% of each run, Pallas kernels for 0% -> 0%
where the time goes in v1:
time: 105 us; the launch traced here: 104 us
  Pallas kernels  98.7 us (94%)
  local copies, waits for them, and re-layouts  5.54 us (5%)
    pallas_call x1, Pallas kernels, local_step(): pl.pallas_call(kernel, out_shape=jax.ShapeDtypeStruct((R, QD), BF16), in_...  98.7 us
    unnamed x4, local copies, waits for them, and re-layouts  5.54 us

profile of v1, /device:TPU:1, one launch (start us, length us, event | category | flops | bytes accessed | tf_op | source)
XLA Modules:
  0.0 104.3 jit_solution(7358350763135780907)
XLA Ops:
  0.0 1.3 %copy.18 = bf16[3,8,2,128]{3,1,2,0:T(8,128)(2,1)} copy(bf16[3,8,2,128]{3,2,1,0:T(2,128)(2,1)} %bitcast.7) | data formatting | bytes 24576
  1.3 1.4 %copy.14.ids = s32[24,2]{1,0:T(8,128)} copy(s32[24,2]{0,1:T(2,128)} %param.19) | data formatting | bytes 384 | tf_op args[6]
  2.7 1.4 %copy.15.gate_w = f32[24,2]{1,0:T(8,128)} copy(f32[24,2]{0,1:T(2,128)} %param.20) | data formatting | bytes 384 | tf_op args[7]
  4.0 98.7 %decode_layer.1 = bf16[24,1536]{1,0:T(8,128)(2,1)} custom-call(s32[24]{0:T(128)} %lengths.1, s32[4]{0:T(128)} %slot_expert.1, bf16[24,768]{1,0:T(8,128)(2,1)} %query.1, bf16[24,256]{1,0:T(8,128)(2,1)} %bitcast.5, bf16[24,6144]{1,0:T(8,128)(2,1)} %residual.1, s32[24,2]{1,0:T(8,128)} %copy.14.ids, f32[24,2]{1,0:T(8,128)} %copy.15.gate_w, ...), custom_call_target="tpu_custom_call" | custom-call | tf_op jit(solution)/shard_map/decode_layer/pallas_call | solution.py:474
  102.8 1.5 %copy.20 = bf16[24,1536]{1,0:T(8,128)(2,1)} copy(bf16[24,1536]{1,0:T(8,128)(2,1)} %decode_layer.1) | data formatting | bytes 147456

commit v2 on v1

v2 whole, which is shorter than its diff:
```python
import jax
import jax.numpy as jnp
from jax import lax
from jax.experimental import pallas as pl
from jax.experimental.pallas import tpu as pltpu
from jax.sharding import PartitionSpec as P

MESH = pl.DeviceIdType.MESH
F32 = jnp.float32
BF16 = jnp.bfloat16

HD = 128
HEADS = 6
R = 24
R2 = 48
CACHE = 512
D = 6144
QD = 1536
W = 256
SEMS = 93
SENDS = 18

STREAMS = (("x", "y", "z"), ("y", "z", "x"), ("z", "x", "y"))
FORWARD_UP = (0, 3)
FORWARD_DOWN = (1, 2)


def wrap(v):
    return lax.rem(v + 4, 4)


def kernel(
    lengths, slot_expert, query, new_kv, residual, ids, gate_w, gain, cache, out_proj, w_gate, w_up, w_down,
    out,
    k_buf, v_buf, op_buf, wg, wu, wd, q_pad, kn, vn, scores, attn_out,
    info_pad, info, res_send, res_recv, z_send, z_recv, z_sib, hidden,
    x_all, ssum, acc_g, acc_u, act,
    part, d2_in, plane_in, row_out, row_in, row_own, blk_out, blk_in, fin_send, fin,
    send_sems, recv_sems, local_sems,
):
    attn = lax.axis_index("attn")
    me = {"y": attn // 2, "c": lax.rem(attn, 2), "z": lax.axis_index("tp"), "x": lax.axis_index("exp")}
    c, other = me["c"], 1 - me["c"]

    def device(c=None, **steps):
        at = dict(me)
        for axis, step in steps.items():
            at[axis] = wrap(at[axis] + step)
        if c is not None:
            at["c"] = c
        return (at["y"] * 2 + at["c"], at["z"], at["x"])

    sibling = device(c=other)

    def local(src, dst, i):
        return pltpu.make_async_copy(src, dst, local_sems.at[i])

    k_copies = [local(cache.at[pl.ds(i * 6, 6), 0], k_buf.at[pl.ds(i * 6, 6)], i) for i in range(4)]
    v_copies = [local(cache.at[pl.ds(i * 6, 6), 1], v_buf.at[pl.ds(i * 6, 6)], 4 + i) for i in range(4)]
    op_copies = {
        j: local(out_proj.at[:, pl.ds(pl.multiple_of(wrap(me["z"] + j) * QD, QD), QD)], op_buf.at[j], 8 + j)
        for j in (2, 1, 3, 0)
    }
    w_copies = [local(w_gate.at[0], wg, 12), local(w_up.at[0], wu, 13)]

    def down_columns(z, s, h):
        return w_down.at[0, :, pl.ds(pl.multiple_of(z * QD + s * 512 + h * W, W), W)]

    def down_rows(core):
        return pl.ds(pl.multiple_of(core * W, W), W)

    for cp in k_copies + v_copies:
        cp.start()
    for j in (2, 1, 3, 0):
        op_copies[j].start()

    barrier = pltpu.get_barrier_semaphore()
    partners = [device(c=k, z=j) for j in (1, 2, 3) for k in (0, 1)] + [sibling]
    partners += [device(**{a: j}) for a in ("x", "y") for j in (1, 2, 3)]
    for p in partners:
        pl.semaphore_signal(barrier, inc=1, device_id=p, device_id_type=MESH)

    table, classes = {}, {}

    def sem(key):
        if key not in table:
            table[key] = len(table)
            assert len(table) <= SEMS
        return recv_sems.at[table[key]]

    def left(kind):
        if kind not in classes:
            classes[kind] = len(classes)
            assert len(classes) <= SENDS
        return send_sems.at[classes[kind]]

    def send(src, dst, kind, key, to):
        pltpu.make_async_remote_copy(
            src_ref=src, dst_ref=dst, send_sem=left(kind), recv_sem=sem(key), device_id=to, device_id_type=MESH
        ).start()

    def arrived(dst, key):
        pltpu.make_async_remote_copy(
            src_ref=dst, dst_ref=dst, send_sem=send_sems.at[0], recv_sem=sem(key),
            device_id=sibling, device_id_type=MESH,
        ).wait_recv()

    def drain(src, kind):
        pltpu.make_async_remote_copy(
            src_ref=src, dst_ref=src, send_sem=left(kind), recv_sem=recv_sems.at[0],
            device_id=sibling, device_id_type=MESH,
        ).wait_send()

    info_pad[...] = jnp.zeros_like(info_pad)
    for s in range(4):
        hit = jnp.where(ids[...] == slot_expert[s], gate_w[...], 0.0)
        info_pad[s : s + 1, :R] = jnp.sum(hit, axis=0, keepdims=True)
    info[c, me["y"], me["x"]] = info_pad[...].T[:R]

    def res_part(h):
        return jnp.concatenate(
            [residual[:, pl.ds(pl.multiple_of(me["z"] * QD + s * 512 + h * W, W), W)] for s in range(3)], axis=1
        ).astype(F32)

    res_send[...] = res_part(other)

    for h in range(8):
        if h < HEADS:
            q_pad[pl.ds(h, R, stride=8), :] = query[:, h * HD : (h + 1) * HD].astype(F32)
        else:
            q_pad[pl.ds(h, R, stride=8), :] = jnp.zeros((R, HD), F32)
        kn[pl.ds(h, R, stride=8), :] = new_kv[:, 0, :].astype(F32)
        vn[pl.ds(h, R, stride=8), :] = new_kv[:, 1, :].astype(F32)
    scale = HD ** (-0.5)
    position = lax.broadcasted_iota(jnp.int32, (8, CACHE), 1)

    for i in range(4):
        k_copies[i].wait()
        for r in range(i * 6, i * 6 + 6):
            s = lax.dot_general(
                q_pad[r * 8 : r * 8 + 8, :].astype(BF16), k_buf[r], (((1,), (1,)), ((), ())),
                preferred_element_type=F32,
            ) * scale
            scores[r * 8 : r * 8 + 8, :] = jnp.where(position < lengths[r], s, -1e30)
    own_score = jnp.sum(q_pad[...] * kn[...], axis=1, keepdims=True) * scale
    raw = scores[...]
    top = jnp.maximum(jnp.max(raw, axis=1, keepdims=True), own_score)
    weight = jnp.exp(raw - top)
    own_weight = jnp.exp(own_score - top)
    total = jnp.sum(weight, axis=1, keepdims=True) + own_weight
    scores[...] = weight / total
    own_prob = (own_weight / total).astype(BF16).astype(F32)
    for i in range(4):
        v_copies[i].wait()
        for r in range(i * 6, i * 6 + 6):
            attn_out[r * 8 : r * 8 + 8, :] = jnp.dot(
                scores[r * 8 : r * 8 + 8, :].astype(BF16), v_buf[r], preferred_element_type=F32
            )
    attn_out[...] = attn_out[...] + own_prob * vn[...]
    attended = jnp.concatenate([attn_out[pl.ds(h, R, stride=8), :] for h in range(HEADS)], axis=1).astype(BF16)

    def pack(v):
        return jnp.concatenate([v[:, :384], v[:, 384:]], axis=0).astype(BF16)

    def unpack(v):
        v = v.astype(F32)
        return jnp.concatenate([v[:R], v[R:]], axis=1)

    own_term = None
    for j in (2, 1, 3, 0):
        op_copies[j].wait()
        term = jnp.dot(attended, op_buf[j], preferred_element_type=F32)
        halves = [
            jnp.concatenate([term[:, s * 512 + h * W : s * 512 + (h + 1) * W] for s in range(3)], axis=1)
            for h in range(2)
        ]
        if j == 2:
            pl.semaphore_wait(barrier, len(partners))
            send(res_send, res_recv, "res", "res", sibling)
        if j:
            for h in range(2):
                z_send[j - 1, h] = pack(halves[h])
                send(z_send.at[j - 1, h], z_recv.at[j - 1, c], "z", "z", device(c=h, z=j))
        else:
            hidden[0] = halves[0]
            hidden[1] = halves[1]
            own_term = hidden[c]
            z_sib[0] = pack(hidden[other])
            send(z_sib.at[0], z_sib.at[1], "zs", "zs", sibling)

    for cp in w_copies:
        cp.start()
    for j in (1, 3, 2):
        spot = info.at[c, me["y"], me["x"]]
        send(spot, spot, "ix", "ix", device(x=j))
    for z in range(4):
        for s in range(3):
            send(down_columns(z, s, other), wd.at[z, s, down_rows(c)], "wd", "wd", sibling)
            local(down_columns(z, s, c), wd.at[z, s, down_rows(c)], 14).start()

    acc_g[...] = jnp.zeros_like(acc_g)
    acc_u[...] = jnp.zeros_like(acc_u)
    ssum[...] = jnp.zeros_like(ssum)

    arrived(res_recv, "res")
    arrived(z_sib.at[1], "zs")
    mine = own_term + res_part(c)
    theirs = res_recv[...] + unpack(z_sib[1])
    arrived(z_recv, "z")
    for j in range(3):
        mine = mine + unpack(z_recv[j, c])
        theirs = theirs + unpack(z_recv[j, other])
    hidden[c] = mine
    hidden[other] = theirs
    sent = jnp.concatenate([hidden[0], hidden[1]], axis=0).astype(BF16)

    place = [tuple(me[a] for a in axes) for axes in STREAMS]

    def own_blocks(core, s, n):
        return x_all.at[core, s, 0, 0, pl.ds(0, n)]

    for s, (a1, a2, a3) in enumerate(STREAMS):
        p1, p2, p3 = place[s]
        x_all[c, s, p3, p2, p1] = sent[:, s * W : (s + 1) * W]
        for j in (1, 3, 2):
            spot = x_all.at[c, s, p3, p2, p1]
            send(spot, spot, "g1", ("g1", s), device(**{a1: j}))

    def row(s, j3, j2, core):
        _, p2, p3 = place[s]
        return x_all.at[core, s, wrap(p3 + j3), wrap(p2 + j2)]

    def share_key(s, j3, j2):
        if j3 == 0:
            return ("gs", s, 0, j2 == 0)
        if j3 == 2:
            return ("gs", s, 2, j2 == 2)
        return ("gs", s, 1, j2 in (0, 1))

    def share(s, j3, j2):
        spot = row(s, j3, j2, c)
        send(spot, spot, "gs", share_key(s, j3, j2), sibling)

    def shared(j3, j2):
        for s in range(3):
            key = share_key(s, j3, j2)
            if j3 == 1:
                size = x_all.at[other, s, 0]
            elif key[3]:
                size = x_all.at[other, s, 0, 0]
            else:
                size = x_all.at[other, s, 0, pl.ds(0, 3)]
            arrived(size, key)

    def out3(s, j2):
        spot = row(s, 0, j2, c)
        for j in (1, 3):
            send(spot, spot, "g3", ("g3", s, j2), device(**{STREAMS[s][2]: j}))
        share(s, 0, j2)

    def take1():
        for s, (a1, a2, a3) in enumerate(STREAMS):
            arrived(x_all.at[c, s, 0, 0, pl.ds(0, 3)], ("g1", s))
            spot = row(s, 0, 0, c)
            for j in (1, 3, 2):
                send(spot, spot, "g2", ("g2", s, j), device(**{a2: j}))
            out3(s, 0)

    def take2(j):
        for s in range(3):
            arrived(row(s, 0, -j, c), ("g2", s, j))
            out3(s, 4 - j)

    def take3(j2):
        for s in range(3):
            arrived(x_all.at[c, s, 0, pl.ds(0, 2)], ("g3", s, j2))
            for j in (1, 3):
                spot = row(s, -j, j2, c)
                if j2 in (FORWARD_UP if j == 1 else FORWARD_DOWN):
                    send(spot, spot, "g3", ("g4", s, j2), device(**{STREAMS[s][2]: j}))
                share(s, 4 - j, j2)

    def take4(j2):
        for s in range(3):
            spot = row(s, 2, j2, c)
            arrived(spot, ("g4", s, j2))
            share(s, 2, j2)

    def multiply(xs, k0, spot):
        g = u = sq = None
        for h in range(2):
            x = xs[h].reshape(4 * R2, W).astype(F32)
            k = k0 + h
            part_sq = x * x
            part_sq = part_sq[:, :128] + part_sq[:, 128:]
            xb = (x * gain[k]).astype(BF16)
            rows = pl.ds(pl.multiple_of(k * W, W), W)
            part_g = jnp.dot(xb, wg[rows, :], preferred_element_type=F32)
            part_u = jnp.dot(xb, wu[rows, :], preferred_element_type=F32)
            g = part_g if g is None else g + part_g
            u = part_u if u is None else u + part_u
            sq = part_sq if sq is None else sq + part_sq
        acc_g[spot] = acc_g[spot] + g.reshape(4, R2, W)
        acc_u[spot] = acc_u[spot] + u.reshape(4, R2, W)
        ssum[spot] = ssum[spot] + sq.reshape(4, R2, 128)

    def rows_01(count, at):
        def step(t, carry):
            j3, j2 = at(t)
            for s in range(2):
                q, i = wrap(place[s][2] + j3), wrap(place[s][1] + j2)
                xs = [x_all[h, s, q, i] for h in range(2)]
                multiply(xs, (q if s == 0 else i) * 6 + s * 2, (i,) if s == 0 else (slice(None), q))
            return carry

        lax.fori_loop(0, count, step, 0)

    def planes_2(count, at):
        def step(t, carry):
            q, i = wrap(place[2][2] + at(t // 4)), lax.rem(t, 4)
            xs = [x_all[h, 2, q, :, i] for h in range(2)]
            multiply(xs, i * 6 + 4, (q,))
            return carry

        lax.fori_loop(0, 4 * count, step, 0)

    take1()
    for cp in w_copies:
        cp.wait()
    shared(0, 0)
    rows_01(1, lambda t: (0, 0))
    take2(1)
    take2(3)
    take2(2)
    take3(0)
    arrived(info.at[c, 0, pl.ds(0, 3)], "ix")
    for j in (1, 3, 2):
        spot = info.at[c, me["y"]]
        send(spot, spot, "iy", "iy", device(y=j))
    shared(0, 1)
    rows_01(2, lambda t: (0, 1 + 2 * t))
    take3(1)
    rows_01(1, lambda t: (0, 2))
    planes_2(1, lambda n: 0)
    take3(3)
    shared(1, 0)
    rows_01(4, lambda t: (1 + 2 * lax.rem(t, 2), t // 2))
    take3(2)
    take4(0)
    take4(1)
    arrived(info.at[c, pl.ds(0, 3)], "iy")
    send(info.at[c], info.at[c], "ic", "ic", sibling)
    shared(1, 3)
    rows_01(4, lambda t: (1 + 2 * lax.rem(t, 2), 3 - t // 2))
    take4(3)
    planes_2(2, lambda n: 1 + 2 * n)
    take4(2)
    shared(2, 0)
    rows_01(3, lambda t: (2, t + t // 2))
    shared(2, 2)
    rows_01(1, lambda t: (2, 2))
    planes_2(1, lambda n: 2)

    arrived(info.at[other], "ic")
    lane4 = lax.broadcasted_iota(jnp.int32, (4, R2, 128), 2)

    def activate(i, carry):
        both = jnp.concatenate([info[0, i], info[1, i]], axis=1)
        chosen = jnp.sum(jnp.where(lane4 == me["x"], both, 0.0), axis=2, keepdims=True)
        inv = lax.rsqrt(jnp.sum(ssum[i], axis=2, keepdims=True) / D + 1e-05)
        g = acc_g[i] * inv
        u = acc_u[i] * inv
        act[c, i] = (g / (1.0 + jnp.exp(-g)) * u * chosen).astype(BF16)
        send(act.at[c, i], act.at[c, i], "act", "act", sibling)
        return carry

    lax.fori_loop(0, 4, activate, 0)
    local(wd.at[:, :, down_rows(0)], wd.at[:, :, down_rows(0)], 14).wait()
    arrived(wd.at[:, :, down_rows(0)], "wd")
    arrived(act.at[other], "act")

    def down(s, j3):
        q = wrap(place[s][2] + j3)

        def step(i, carry):
            pick = (i,) if s == 0 else ((slice(None), q) if s == 1 else (q,))
            a = jnp.concatenate([act[(h,) + pick].reshape(4 * R2, W) for h in range(2)], axis=1)
            w = wd[q if s == 0 else i, s]
            y = jnp.dot(a, w, preferred_element_type=F32).reshape(4, R2, W).astype(BF16)
            if s == 2:
                part[s, j3, :, i] = y
            else:
                part[s, j3, i] = y
            return carry

        lax.fori_loop(0, 4, step, 0)

    def second(s, j2):
        return wrap(place[s][1] + j2)

    def send_far(s):
        for j2 in (2, 3, 1, 0):
            j = 1 if j2 in FORWARD_UP else 3
            r = second(s, j2)
            send(part.at[s, 2, r], d2_in.at[s, r], "r4", ("r4", s, j2), device(**{STREAMS[s][2]: j}))

    def send_near(s, j, j2):
        r = second(s, j2)
        send(part.at[s, j, r], plane_in.at[s, j // 2, r], "r3", ("r3", s, j2), device(**{STREAMS[s][2]: j}))

    for s in range(3):
        down(s, 2)
        send_far(s)
    for s in range(3):
        down(s, 1)
        for j2 in (2, 1):
            send_near(s, 1, j2)
        down(s, 3)
        for j2 in (3, 0):
            send_near(s, 3, j2)
    for s in range(3):
        down(s, 0)
    for j2 in (2, 3, 1, 0):
        j = 1 if j2 in FORWARD_UP else 3
        for s in range(3):
            r = second(s, j2)
            arrived(d2_in.at[s, r], ("r4", s, j2))
            part[s, j, r] = (part[s, j, r].astype(F32) + d2_in[s, r].astype(F32)).astype(BF16)
            send_near(s, j, j2)

    for j2 in (2, 3, 1, 0):
        for s in range(3):
            r = second(s, j2)
            arrived(plane_in.at[s, :, r], ("r3", s, j2))
            v = part[s, 0, r].astype(F32) + plane_in[s, 0, r].astype(F32) + plane_in[s, 1, r].astype(F32)
            if j2:
                row_out[s, j2 - 1] = v.astype(BF16)
                send(row_out.at[s, j2 - 1], row_in.at[s, j2 - 1], "r2", ("r2", s), device(**{STREAMS[s][1]: j2}))
            else:
                row_own[s] = v
    for s in range(3):
        arrived(row_in.at[s], ("r2", s))
        row_own[s] = row_own[s] + (
            row_in[s, 0].astype(F32) + row_in[s, 1].astype(F32) + row_in[s, 2].astype(F32)
        )
        for j1 in (2, 1, 3):
            blk_out[s, j1 - 1] = row_own[s, wrap(place[s][0] + j1)].astype(BF16)
            send(blk_out.at[s, j1 - 1], blk_in.at[s, j1 - 1], "r1", ("r1", s), device(**{STREAMS[s][0]: j1}))

    drain(res_send, "res")
    drain(z_send, "z")
    drain(z_sib.at[0], "zs")
    drain(info.at[c, 0, pl.ds(0, 3)], "ix")
    drain(info.at[c, pl.ds(0, 3)], "iy")
    drain(info.at[c], "ic")
    drain(wd.at[:, :, down_rows(0)], "wd")
    drain(x_all.at[c, :, 0, 0, pl.ds(0, 3)], "g1")
    drain(x_all.at[c, :, 0, pl.ds(0, 3)], "g2")
    drain(x_all.at[c, :, pl.ds(0, 3)], "g3")
    drain(x_all.at[c], "gs")
    drain(act.at[c], "act")
    drain(d2_in, "r4")
    drain(plane_in, "r3")
    drain(row_out, "r2")

    for s in range(3):
        v = row_own[s, place[s][0]]
        arrived(blk_in.at[s], ("r1", s))
        for j in range(3):
            v = v + blk_in[s, j].astype(F32)
        for k in range(2):
            fin_send[k, s] = hidden[k, :, s * W : (s + 1) * W] + v[k * R : (k + 1) * R]
        send(fin_send.at[other, s], fin.at[s], "fin", "fin", sibling)
    drain(blk_out, "r1")
    arrived(fin, "fin")
    drain(fin, "fin")
    for s in range(3):
        fin_send[other, s] = fin[s]
        for h in range(2):
            out[:, s * 512 + h * W : s * 512 + (h + 1) * W] = fin_send[h, s].astype(BF16)


def local_step(
    new_query, new_kv, kv_cache, lengths, residual, out_proj, expert_ids, gate_weights, slot_expert, moe_gain,
    w_gate, w_up, w_down,
):
    vmem = pl.BlockSpec(memory_space=pltpu.VMEM)
    smem = pl.BlockSpec(memory_space=pltpu.SMEM)
    anywhere = pl.BlockSpec(memory_space=pl.ANY)
    v = pltpu.VMEM
    return pl.pallas_call(
        kernel,
        out_shape=jax.ShapeDtypeStruct((R, QD), BF16),
        in_specs=[smem, smem] + [vmem] * 6 + [anywhere] * 5,
        out_specs=vmem,
        scratch_shapes=[
            v((R, CACHE, HD), BF16),
            v((R, CACHE, HD), BF16),
            v((4, HEADS * HD, QD), BF16),
            v((D, W), BF16),
            v((D, W), BF16),
            v((4, 3, 2 * W, W), BF16),
            v((R * 8, HD), F32),
            v((R * 8, HD), F32),
            v((R * 8, HD), F32),
            v((R * 8, CACHE), F32),
            v((R * 8, HD), F32),
            v((128, 128), F32),
            v((2, 4, 4, R, 128), F32),
            v((R, 3 * W), F32),
            v((R, 3 * W), F32),
            v((3, 2, R2, 384), BF16),
            v((3, 2, R2, 384), BF16),
            v((2, R2, 384), BF16),
            v((2, R, 3 * W), F32),
            v((2, 3, 4, 4, 4, R2, W), BF16),
            v((4, 4, R2, 128), F32),
            v((4, 4, R2, W), F32),
            v((4, 4, R2, W), F32),
            v((2, 4, 4, R2, W), BF16),
            v((3, 4, 4, 4, R2, W), BF16),
            v((3, 4, 4, R2, W), BF16),
            v((3, 2, 4, 4, R2, W), BF16),
            v((3, 3, 4, R2, W), BF16),
            v((3, 3, 4, R2, W), BF16),
            v((3, 4, R2, W), F32),
            v((3, 3, R2, W), BF16),
            v((3, 3, R2, W), BF16),
            v((2, 3, R, W), F32),
            v((3, R, W), F32),
            pltpu.SemaphoreType.DMA((SENDS,)),
            pltpu.SemaphoreType.DMA((SEMS,)),
            pltpu.SemaphoreType.DMA((15,)),
        ],
        compiler_params=pltpu.CompilerParams(
            collective_id=0, has_side_effects=True, vmem_limit_bytes=62 * 2**20
        ),
        name="decode_layer",
    )(
        lengths, slot_expert, new_query, new_kv, residual, expert_ids.T, gate_weights.T,
        moe_gain.reshape(D // W, 1, W), kv_cache, out_proj, w_gate, w_up, w_down,
    )


def solution(mesh):
    placed = (
        P(("attn", "exp"), "tp"),
        P(("attn", "exp"), None, "tp"),
        P(("attn", "exp"), None, None, "tp"),
        P(("attn", "exp")),
        P(("attn", "exp"), None),
        P("tp", None),
        P(("attn", "exp"), None),
        P(("attn", "exp"), None),
        P(),
        P(),
        P("exp", None, ("attn", "tp")),
        P("exp", None, ("attn", "tp")),
        P("exp", ("attn", "tp"), None),
    )
    return jax.shard_map(
        local_step, mesh=mesh, in_specs=placed, out_specs=P(("attn", "exp"), "tp"), check_vma=False
    )
```

time: 105 us -> 82.1 us (0.78)
  Pallas kernels: 98.7 us -> 80.4 us
  local copies, waits for them, and re-layouts: 5.54 us -> 1.52 us
    pallas_call x1, Pallas kernels: 98.7 us -> 80.4 us  [local_step(): pl.pallas_call(kernel, out_shape=jax.ShapeDtypeStruct((R, QD), BF16), in_...]
    unnamed x4 -> x1, local copies, waits for them, and re-layouts: 5.54 us -> 1.52 us
where the time goes in v2:
time: 82.1 us; the launch traced here: 81.9 us
  Pallas kernels  80.4 us (98%)
  local copies, waits for them, and re-layouts  1.52 us (2%)
    pallas_call x1, Pallas kernels, local_step(): pl.pallas_call(kernel, out_shape=jax.ShapeDtypeStruct((R, QD), BF16), in_...  80.4 us

profile of v2, /device:TPU:1, one launch (start us, length us, event | category | flops | bytes accessed | tf_op | source)
XLA Modules:
  0.0 81.9 jit_solution(18396842430702025394)
XLA Ops:
  0.0 80.4 %decode_layer.1 = bf16[24,1536]{1,0:T(8,128)(2,1)} custom-call(s32[24]{0:T(128)} %lengths.1, s32[4]{0:T(128)} %slot_expert.1, bf16[24,768]{1,0:T(8,128)(2,1)} %query.1, bf16[24,2,128]{2,1,0:T(2,128)(2,1)} %new_kv.1, bf16[24,6144]{1,0:T(8,128)(2,1)} %residual.1, s32[2,24]{1,0:T(2,128)} %bitcast.4, f32[2,24]{1,0:T(2,128)} %bitcast.5, f32[24,1,256]{2,1,0:T(1,128)} %bitcast.3, ...), custom_call_target="tpu_custom_call" | custom-call | tf_op jit(solution)/shard_map/decode_layer/pallas_call | solution.py:491
  80.4 1.5 %copy.15 = bf16[24,1536]{1,0:T(8,128)(2,1)} copy(bf16[24,1536]{1,0:T(8,128)(2,1)} %decode_layer.1) | data formatting | bytes 147456

commit v3 on v0

v3 whole, which is shorter than its diff:
```python
import jax
import jax.numpy as jnp
from jax import lax
from jax.experimental import pallas as pl
from jax.experimental.pallas import tpu as pltpu
from jax.sharding import PartitionSpec as P

MESH = pl.DeviceIdType.MESH
F32 = jnp.float32
BF16 = jnp.bfloat16

HD = 128
HEADS = 6
R = 24
CACHE = 512
D = 6144
QD = 1536
W = 256
SEMS = 44
SENDS = 20
PARTS = ((0, R),)
CHUNK = 6

STREAMS = (("x", "y", "z"), ("y", "z", "x"), ("z", "x", "y"))
FORWARD_UP = (0, 3)
FORWARD_DOWN = (1, 2)


def wrap(v):
    return lax.rem(v + 4, 4)


def common_scratch():
    v = pltpu.VMEM
    return dict(
        k_buf=v((R, CACHE, HD), BF16),
        v_buf=v((R, CACHE, HD), BF16),
        op_buf=v((4, HEADS * HD, QD), BF16),
        wg=v((D, W), BF16),
        wu=v((D, W), BF16),
        wd=v((4, 3, 2 * W, W), BF16),
        q_pad=v((R * 8, HD), F32),
        kn=v((R * 8, HD), F32),
        vn=v((R * 8, HD), F32),
        scores=v((R * 8, CACHE), F32),
        attn_out=v((R * 8, HD), F32),
        info_pad=v((128, 128), F32),
        info=v((2, 4, 4, R, 128), F32),
        res_send=v((R, 3 * W), F32),
        res_recv=v((R, 3 * W), F32),
        hidden=v((2, R, 3 * W), F32),
        result=v((R, QD), F32),
        send_sems=pltpu.SemaphoreType.DMA((SENDS,)),
        recv_sems=pltpu.SemaphoreType.DMA((SEMS,)),
        local_sems=pltpu.SemaphoreType.DMA((7 + 2 * (R // CHUNK),)),
    )


def part_scratch(n):
    v, b = pltpu.VMEM, 2 * n
    return dict(
        z_send=v((3, 2, b, 384), BF16),
        z_recv=v((3, 2, b, 384), BF16),
        z_sib=v((2, b, 384), BF16),
        z_own=v((2, n, 3 * W), F32),
        x_all=v((2, 3, 4, 4, 4, b, W), BF16),
        ssum=v((4, 4, b, 128), F32),
        acc_g=v((4, 4, b, W), F32),
        acc_u=v((4, 4, b, W), F32),
        act=v((2, 4, 4, b, W), BF16),
        part=v((3, 4, 4, 4, b, W), BF16),
        d2_in=v((3, 4, 4, b, W), BF16),
        plane_in=v((3, 2, 4, 4, b, W), BF16),
        row_out=v((3, 3, 4, b, W), BF16),
        row_in=v((3, 3, 4, b, W), BF16),
        row_own=v((3, 4, b, W), F32),
        blk_out=v((3, 3, b, W), BF16),
        blk_in=v((3, 3, b, W), BF16),
        fin_send=v((2, 3, n, W), F32),
        fin=v((3, n, W), F32),
    )


def kernel(*refs):
    (lengths, slot_expert, query, new_kv, residual, ids, gate_w, gain, cache, out_proj, w_gate, w_up, w_down, out) = refs[:14]
    names = common_scratch()
    m = dict(zip(names, refs[14:]))
    at = 14 + len(names)
    buffers = []
    for _, n in PARTS:
        names = part_scratch(n)
        buffers.append(dict(zip(names, refs[at:])))
        at += len(names)
    k_buf, v_buf, op_buf, wg, wu, wd = (m[k] for k in ("k_buf", "v_buf", "op_buf", "wg", "wu", "wd"))
    q_pad, kn, vn, scores, attn_out = (m[k] for k in ("q_pad", "kn", "vn", "scores", "attn_out"))
    info, res_send, res_recv, hidden, result = (m[k] for k in ("info", "res_send", "res_recv", "hidden", "result"))
    info_pad, send_sems, recv_sems, local_sems = (m[k] for k in ("info_pad", "send_sems", "recv_sems", "local_sems"))

    attn = lax.axis_index("attn")
    me = {"y": attn // 2, "c": lax.rem(attn, 2), "z": lax.axis_index("tp"), "x": lax.axis_index("exp")}
    c, other = me["c"], 1 - me["c"]
    place = [tuple(me[a] for a in axes) for axes in STREAMS]

    def device(c=None, **steps):
        at = dict(me)
        for axis, step in steps.items():
            at[axis] = wrap(at[axis] + step)
        if c is not None:
            at["c"] = c
        return (at["y"] * 2 + at["c"], at["z"], at["x"])

    sibling = device(c=other)

    def local(src, dst, i):
        return pltpu.make_async_copy(src, dst, local_sems.at[i])

    op_copies = {
        j: local(out_proj.at[:, pl.ds(pl.multiple_of(wrap(me["z"] + j) * QD, QD), QD)], op_buf.at[j], j)
        for j in (2, 1, 3, 0)
    }
    w_copies = [local(w_gate.at[0], wg, 4), local(w_up.at[0], wu, 5)]
    k_copies, v_copies = [], []
    for i in range(R // CHUNK):
        some = pl.ds(i * CHUNK, CHUNK)
        k_copies.append(local(cache.at[some, 0], k_buf.at[some], 7 + 2 * i))
        v_copies.append(local(cache.at[some, 1], v_buf.at[some], 8 + 2 * i))

    def down_columns(z, s, h):
        return w_down.at[0, :, pl.ds(pl.multiple_of(z * QD + s * 512 + h * W, W), W)]

    def down_rows(core):
        return pl.ds(pl.multiple_of(core * W, W), W)

    for cp in k_copies + v_copies:
        cp.start()
    for j in (2, 1, 3, 0):
        op_copies[j].start()

    barrier = pltpu.get_barrier_semaphore()
    partners = [device(c=k, z=j) for j in (1, 2, 3) for k in (0, 1)] + [sibling]
    partners += [device(**{a: j}) for a in ("x", "y") for j in (1, 2, 3)]
    for p in partners:
        pl.semaphore_signal(barrier, inc=1, device_id=p, device_id_type=MESH)

    table, classes = {}, {}

    def sem(key):
        if key not in table:
            table[key] = len(table)
            assert len(table) <= SEMS
        return recv_sems.at[table[key]]

    def left(kind):
        if kind not in classes:
            classes[kind] = len(classes)
            assert len(classes) <= SENDS
        return send_sems.at[classes[kind]]

    def send(src, dst, kind, key, to):
        pltpu.make_async_remote_copy(
            src_ref=src, dst_ref=dst, send_sem=left(kind), recv_sem=sem(key), device_id=to, device_id_type=MESH
        ).start()

    def arrived(dst, key):
        pltpu.make_async_remote_copy(
            src_ref=dst, dst_ref=dst, send_sem=send_sems.at[0], recv_sem=sem(key),
            device_id=sibling, device_id_type=MESH,
        ).wait_recv()

    def drain(src, kind):
        pltpu.make_async_remote_copy(
            src_ref=src, dst_ref=src, send_sem=left(kind), recv_sem=recv_sems.at[0],
            device_id=sibling, device_id_type=MESH,
        ).wait_send()

    info_pad[...] = jnp.zeros_like(info_pad)
    for s in range(4):
        hit = jnp.where(ids[...] == slot_expert[s], gate_w[...], 0.0)
        info_pad[s : s + 1, :R] = jnp.sum(hit, axis=0, keepdims=True)
    info[c, me["y"], me["x"]] = info_pad[...].T[:R]

    def res_part(h):
        return jnp.concatenate(
            [residual[:, pl.ds(pl.multiple_of(me["z"] * QD + s * 512 + h * W, W), W)] for s in range(3)], axis=1
        ).astype(F32)

    res_send[...] = res_part(other)
    hidden[c] = res_part(c)
    for h in range(8):
        if h < HEADS:
            q_pad[pl.ds(h, R, stride=8), :] = query[:, h * HD : (h + 1) * HD].astype(F32)
        else:
            q_pad[pl.ds(h, R, stride=8), :] = jnp.zeros((R, HD), F32)
        kn[pl.ds(h, R, stride=8), :] = new_kv[:, 0, :].astype(F32)
        vn[pl.ds(h, R, stride=8), :] = new_kv[:, 1, :].astype(F32)

    def begin_links():
        pl.semaphore_wait(barrier, len(partners))
        send(res_send, res_recv, "res", "res", sibling)

    def info_1():
        for j in (1, 3, 2):
            spot = info.at[c, me["y"], me["x"]]
            send(spot, spot, "ix", "ix", device(x=j))

    def info_2():
        arrived(info.at[c, 0, pl.ds(0, 3)], "ix")
        for j in (1, 3, 2):
            spot = info.at[c, me["y"]]
            send(spot, spot, "iy", "iy", device(y=j))

    def info_3():
        arrived(info.at[c, pl.ds(0, 3)], "iy")
        send(info.at[c], info.at[c], "ic", "ic", sibling)

    def load_weights():
        for cp in w_copies:
            cp.start()
        for z in range(4):
            for s in range(3):
                send(down_columns(z, s, other), wd.at[z, s, down_rows(c)], "wd", "wd", sibling)
                local(down_columns(z, s, c), wd.at[z, s, down_rows(c)], 6).start()

    def pack(v):
        return jnp.concatenate([v[:, :384], v[:, 384:]], axis=0).astype(BF16)

    def flow(t):
        r0, n = PARTS[t]
        b = 2 * n
        p = buffers[t]
        z_send, z_recv, z_sib, z_own = (p[k] for k in ("z_send", "z_recv", "z_sib", "z_own"))
        x_all, ssum, acc_g, acc_u, act = (p[k] for k in ("x_all", "ssum", "acc_g", "acc_u", "act"))
        part, d2_in, plane_in = (p[k] for k in ("part", "d2_in", "plane_in"))
        row_out, row_in, row_own, blk_out, blk_in = (p[k] for k in ("row_out", "row_in", "row_own", "blk_out", "blk_in"))
        fin_send, fin = p["fin_send"], p["fin"]

        scale = HD ** (-0.5)
        position = lax.broadcasted_iota(jnp.int32, (8, CACHE), 1)
        mine8 = slice(r0 * 8, (r0 + n) * 8)
        for r in range(r0, r0 + n):
            if r % CHUNK == 0:
                k_copies[r // CHUNK].wait()
            s = lax.dot_general(
                q_pad[r * 8 : r * 8 + 8, :].astype(BF16), k_buf[r], (((1,), (1,)), ((), ())),
                preferred_element_type=F32,
            ) * scale
            scores[r * 8 : r * 8 + 8, :] = jnp.where(position < lengths[r], s, -1e30)
        own_score = jnp.sum(q_pad[mine8, :] * kn[mine8, :], axis=1, keepdims=True) * scale
        raw = scores[mine8, :]
        top = jnp.maximum(jnp.max(raw, axis=1, keepdims=True), own_score)
        weight = jnp.exp(raw - top)
        own_weight = jnp.exp(own_score - top)
        total = jnp.sum(weight, axis=1, keepdims=True) + own_weight
        scores[mine8, :] = weight / total
        own_prob = (own_weight / total).astype(BF16).astype(F32)
        for r in range(r0, r0 + n):
            if r % CHUNK == 0:
                v_copies[r // CHUNK].wait()
            attn_out[r * 8 : r * 8 + 8, :] = jnp.dot(
                scores[r * 8 : r * 8 + 8, :].astype(BF16), v_buf[r], preferred_element_type=F32
            )
        attn_out[mine8, :] = attn_out[mine8, :] + own_prob * vn[mine8, :]
        attended = jnp.concatenate(
            [attn_out[pl.ds(r0 * 8 + h, n, stride=8), :] for h in range(HEADS)], axis=1
        ).astype(BF16)

        def unpack(v):
            v = v.astype(F32)
            return jnp.concatenate([v[:n], v[n:]], axis=1)

        for j in (2, 1, 3, 0):
            if t == 0:
                op_copies[j].wait()
            term = jnp.dot(attended, op_buf[j], preferred_element_type=F32)
            halves = [
                jnp.concatenate([term[:, s * 512 + h * W : s * 512 + (h + 1) * W] for s in range(3)], axis=1)
                for h in range(2)
            ]
            if j == 2 and t == 0:
                begin_links()
            if j:
                for h in range(2):
                    z_send[j - 1, h] = pack(halves[h])
                    send(z_send.at[j - 1, h], z_recv.at[j - 1, c], ("z", t), ("z", t), device(c=h, z=j))
            else:
                z_own[0] = halves[0]
                z_own[1] = halves[1]
                z_sib[0] = pack(z_own[other])
                send(z_sib.at[0], z_sib.at[1], ("zs", t), ("zs", t), sibling)
        info_1()
        load_weights()
        acc_g[...] = jnp.zeros_like(acc_g)
        acc_u[...] = jnp.zeros_like(acc_u)
        ssum[...] = jnp.zeros_like(ssum)

        def pass_on(s, j):
            p1, p2, p3 = place[s]
            spot = x_all.at[c, s, p3, p2, wrap(p1 - j)]
            for k in (2, 1, 3):
                send(spot, spot, ("g2", t), ("g2", t, k), device(**{STREAMS[s][1]: k}))
            for k in (1, 3):
                send(spot, spot, ("g3", t), ("g3", t, 0), device(**{STREAMS[s][2]: k}))

        if t == 0:
            arrived(res_recv, "res")
            hidden[other] = res_recv[...]
        arrived(z_sib.at[1], ("zs", t))
        rows = slice(r0, r0 + n)
        mine = hidden[c, rows] + z_own[c]
        theirs = hidden[other, rows] + unpack(z_sib[1])
        arrived(z_recv, ("z", t))
        for j in range(3):
            mine = mine + unpack(z_recv[j, c])
            theirs = theirs + unpack(z_recv[j, other])
        hidden[c, rows] = mine
        hidden[other, rows] = theirs
        sent = jnp.concatenate([hidden[0, rows], hidden[1, rows]], axis=0).astype(BF16)
        for s, (a1, a2, a3) in enumerate(STREAMS):
            p1, p2, p3 = place[s]
            x_all[c, s, p3, p2, p1] = sent[:, s * W : (s + 1) * W]
            for j in (2, 1, 3):
                spot = x_all.at[c, s, p3, p2, p1]
                send(spot, spot, ("g1", t), ("g1", t, j), device(**{a1: j}))
        for s in range(3):
            pass_on(s, 0)

        def row(s, j3, j2, core):
            _, p2, p3 = place[s]
            return x_all.at[core, s, wrap(p3 + j3), wrap(p2 + j2)]

        def share_key(j3, j2):
            if j3 == 0:
                return ("gs", t, 0, j2 == 0)
            if j3 == 2:
                return ("gs", t, 2, j2 == 2)
            return ("gs", t, 1, j2 in (0, 1))

        def share(s, j3, j2):
            spot = row(s, j3, j2, c)
            send(spot, spot, ("gs", t), share_key(j3, j2), sibling)

        def shared(j3, j2):
            key = share_key(j3, j2)
            if j3 == 1:
                arrived(x_all.at[other, :, 0], key)
            elif key[3]:
                arrived(x_all.at[other, :, 0, 0], key)
            else:
                arrived(x_all.at[other, :, 0, pl.ds(0, 3)], key)

        def take1():
            for j in (1, 3, 2):
                arrived(x_all.at[c, :, 0, 0, 0], ("g1", t, j))
                for s in range(3):
                    pass_on(s, j)
            for s in range(3):
                share(s, 0, 0)

        def take2(j):
            arrived(x_all.at[c, :, 0, 0], ("g2", t, j))
            for s in range(3):
                spot = row(s, 0, 4 - j, c)
                for k in (1, 3):
                    send(spot, spot, ("g3", t), ("g3", t, 4 - j), device(**{STREAMS[s][2]: k}))
                share(s, 0, 4 - j)

        def take3(j2):
            arrived(x_all.at[c, :, 0, pl.ds(0, 2)], ("g3", t, j2))
            for s in range(3):
                for j in (1, 3):
                    spot = row(s, -j, j2, c)
                    half = spot.at[pl.ds(0 if j == 1 else 2, 2)]
                    send(half, half, ("g3", t), ("g4", t, j2), device(**{STREAMS[s][2]: j}))
                    share(s, 4 - j, j2)

        def take4(j2):
            arrived(x_all.at[c, :, 0, 0], ("g4", t, j2))
            for s in range(3):
                share(s, 2, j2)

        def multiply(xs, k0, spots):
            g = u = sq = None
            for h in range(2):
                x = jnp.concatenate([v.reshape(4 * b, W) for v in xs[h]], axis=0).astype(F32)
                k = k0 + h
                part_sq = x * x
                part_sq = part_sq[:, :128] + part_sq[:, 128:]
                xb = (x * gain[k]).astype(BF16)
                weight_rows = pl.ds(pl.multiple_of(k * W, W), W)
                part_g = jnp.dot(xb, wg[weight_rows, :], preferred_element_type=F32)
                part_u = jnp.dot(xb, wu[weight_rows, :], preferred_element_type=F32)
                g = part_g if g is None else g + part_g
                u = part_u if u is None else u + part_u
                sq = part_sq if sq is None else sq + part_sq
            for i, spot in enumerate(spots):
                m4 = slice(i * 4 * b, (i + 1) * 4 * b)
                acc_g[spot] = acc_g[spot] + g[m4].reshape(4, b, W)
                acc_u[spot] = acc_u[spot] + u[m4].reshape(4, b, W)
                ssum[spot] = ssum[spot] + sq[m4].reshape(4, b, 128)

        def rows_01(j3s, j2s):
            qs = [[wrap(place[s][2] + j3) for j3 in j3s] for s in range(2)]
            rs = [[wrap(place[s][1] + j2) for j2 in j2s] for s in range(2)]
            for q in qs[0]:
                multiply([[x_all[h, 0, q, r] for r in rs[0]] for h in range(2)], q * 6, [(r,) for r in rs[0]])
            for r in rs[1]:
                xs = [[x_all[h, 1, q, r] for q in qs[1]] for h in range(2)]
                multiply(xs, r * 6 + 2, [(slice(None), q) for q in qs[1]])

        def planes_2(j3s):
            qs = [wrap(place[2][2] + j3) for j3 in j3s]
            for z in range(4):
                multiply([[x_all[h, 2, q, :, z] for q in qs] for h in range(2)], z * 6 + 4, [(q,) for q in qs])

        take1()
        if t == 0:
            for cp in w_copies:
                cp.wait()
        shared(0, 0)
        rows_01((0,), (0,))
        take2(1)
        take2(3)
        take2(2)
        take3(0)
        info_2()
        shared(0, 1)
        rows_01((0,), (1, 3))
        take3(1)
        rows_01((0,), (2,))
        planes_2((0,))
        take3(3)
        shared(1, 0)
        rows_01((1, 3), (0, 1))
        take3(2)
        take4(0)
        take4(1)
        info_3()
        shared(1, 3)
        rows_01((1, 3), (3, 2))
        take4(3)
        planes_2((1, 3))
        take4(2)
        shared(2, 0)
        rows_01((2,), (0, 1, 3))
        shared(2, 2)
        rows_01((2,), (2,))
        planes_2((2,))

        if t == 0:
            arrived(info.at[other], "ic")
        lane4 = lax.broadcasted_iota(jnp.int32, (4, b, 128), 2)

        def activate(i, carry):
            both = jnp.concatenate([info[0, i, :, rows], info[1, i, :, rows]], axis=1)
            chosen = jnp.sum(jnp.where(lane4 == me["x"], both, 0.0), axis=2, keepdims=True)
            inv = lax.rsqrt(jnp.sum(ssum[i], axis=2, keepdims=True) / D + 1e-05)
            g = acc_g[i] * inv
            u = acc_u[i] * inv
            act[c, i] = (g / (1.0 + jnp.exp(-g)) * u * chosen).astype(BF16)
            send(act.at[c, i], act.at[c, i], ("act", t), ("act", t), sibling)
            return carry

        lax.fori_loop(0, 4, activate, 0, unroll=2)
        if t == 0:
            local(wd.at[:, :, down_rows(0)], wd.at[:, :, down_rows(0)], 6).wait()
            arrived(wd.at[:, :, down_rows(0)], "wd")
        arrived(act.at[other], ("act", t))

        def down(s, j3):
            q = wrap(place[s][2] + j3)

            def step(i, carry):
                pick = (i,) if s == 0 else ((slice(None), q) if s == 1 else (q,))
                a = jnp.concatenate([act[(h,) + pick].reshape(4 * b, W) for h in range(2)], axis=1)
                w = wd[q if s == 0 else i, s]
                y = jnp.dot(a, w, preferred_element_type=F32).reshape(4, b, W).astype(BF16)
                if s == 2:
                    part[s, j3, :, i] = y
                else:
                    part[s, j3, i] = y
                return carry

            lax.fori_loop(0, 4, step, 0, unroll=4)

        def second(s, j2):
            return wrap(place[s][1] + j2)

        def send_far(s):
            for j2 in (2, 3, 1, 0):
                j = 1 if j2 in FORWARD_UP else 3
                r = second(s, j2)
                send(part.at[s, 2, r], d2_in.at[s, r], ("r4", t), ("r4", t, j2), device(**{STREAMS[s][2]: j}))

        def send_near(s, j, j2):
            r = second(s, j2)
            to = device(**{STREAMS[s][2]: j})
            send(part.at[s, j, r], plane_in.at[s, j // 2, r], ("r3", t), ("r3", t, j2), to)

        def add_far(j2):
            j = 1 if j2 in FORWARD_UP else 3
            arrived(d2_in.at[:, 0], ("r4", t, j2))
            for s in range(3):
                r = second(s, j2)
                part[s, j, r] = (part[s, j, r].astype(F32) + d2_in[s, r].astype(F32)).astype(BF16)
                send_near(s, j, j2)

        for s in range(3):
            down(s, 2)
            send_far(s)
        for s in range(3):
            down(s, 1)
            send_near(s, 1, 2)
            down(s, 3)
            send_near(s, 3, 3)
        for s in range(3):
            down(s, 0)
        add_far(2)
        add_far(3)
        for s in range(3):
            send_near(s, 1, 1)
        add_far(1)
        add_far(0)
        for s in range(3):
            send_near(s, 3, 0)
        for j2 in (2, 3, 1, 0):
            arrived(plane_in.at[:, :, 0], ("r3", t, j2))
            for s in range(3):
                r = second(s, j2)
                v = part[s, 0, r].astype(F32) + plane_in[s, 0, r].astype(F32) + plane_in[s, 1, r].astype(F32)
                if j2:
                    row_out[s, j2 - 1] = v.astype(BF16)
                    to = device(**{STREAMS[s][1]: j2})
                    send(row_out.at[s, j2 - 1], row_in.at[s, j2 - 1], ("r2", t), ("r2", t, s), to)
                else:
                    row_own[s] = v
        for s in range(3):
            arrived(row_in.at[s], ("r2", t, s))
            row_own[s] = row_own[s] + (
                row_in[s, 0].astype(F32) + row_in[s, 1].astype(F32) + row_in[s, 2].astype(F32)
            )
            for j1 in (2, 1, 3):
                blk_out[s, j1 - 1] = row_own[s, wrap(place[s][0] + j1)].astype(BF16)
                to = device(**{STREAMS[s][0]: j1})
                send(blk_out.at[s, j1 - 1], blk_in.at[s, j1 - 1], ("r1", t), ("r1", t, s), to)
        drain(z_send, ("z", t))
        drain(z_sib.at[0], ("zs", t))
        drain(x_all.at[c, :, 0, 0, pl.ds(0, 3)], ("g1", t))
        drain(x_all.at[c, :, 0, pl.ds(0, 3)], ("g2", t))
        drain(x_all.at[c, :, pl.ds(0, 3)], ("g3", t))
        drain(x_all.at[c], ("gs", t))
        drain(act.at[c], ("act", t))
        drain(d2_in, ("r4", t))
        drain(plane_in, ("r3", t))
        drain(row_out, ("r2", t))
        for s in range(3):
            v = row_own[s, place[s][0]]
            arrived(blk_in.at[s], ("r1", t, s))
            for j in range(3):
                v = v + blk_in[s, j].astype(F32)
            for k in range(2):
                fin_send[k, s] = hidden[k, rows, s * W : (s + 1) * W] + v[k * n : (k + 1) * n]
            send(fin_send.at[other, s], fin.at[s], ("fin", t), ("fin", t), sibling)
        drain(blk_out, ("r1", t))
        arrived(fin, ("fin", t))
        drain(fin, ("fin", t))
        for s in range(3):
            fin_send[other, s] = fin[s]
            for h in range(2):
                result[rows, s * 512 + h * W : s * 512 + (h + 1) * W] = fin_send[h, s]

    flow(0)
    drain(res_send, "res")
    drain(info.at[c, 0, pl.ds(0, 3)], "ix")
    drain(info.at[c, pl.ds(0, 3)], "iy")
    drain(info.at[c], "ic")
    drain(wd.at[:, :, down_rows(0)], "wd")
    out[...] = result[...].astype(BF16)


def local_step(
    new_query, new_kv, kv_cache, lengths, residual, out_proj, expert_ids, gate_weights, slot_expert, moe_gain,
    w_gate, w_up, w_down,
):
    vmem = pl.BlockSpec(memory_space=pltpu.VMEM)
    smem = pl.BlockSpec(memory_space=pltpu.SMEM)
    anywhere = pl.BlockSpec(memory_space=pl.ANY)
    scratch = list(common_scratch().values())
    for _, n in PARTS:
        scratch += list(part_scratch(n).values())
    return pl.pallas_call(
        kernel,
        out_shape=jax.ShapeDtypeStruct((R, QD), BF16),
        in_specs=[smem, smem] + [vmem] * 6 + [anywhere] * 5,
        out_specs=vmem,
        scratch_shapes=scratch,
        compiler_params=pltpu.CompilerParams(
            collective_id=0, has_side_effects=True, vmem_limit_bytes=62 * 2**20
        ),
        name="decode_layer",
    )(
        lengths, slot_expert, new_query, new_kv, residual, expert_ids.T, gate_weights.T,
        moe_gain.reshape(D // W, 1, W), kv_cache, out_proj, w_gate, w_up, w_down,
    )


def solution(mesh):
    placed = (
        P(("attn", "exp"), "tp"),
        P(("attn", "exp"), None, "tp"),
        P(("attn", "exp"), None, None, "tp"),
        P(("attn", "exp")),
        P(("attn", "exp"), None),
        P("tp", None),
        P(("attn", "exp"), None),
        P(("attn", "exp"), None),
        P(),
        P(),
        P("exp", None, ("attn", "tp")),
        P("exp", None, ("attn", "tp")),
        P("exp", ("attn", "tp"), None),
    )
    return jax.shard_map(
        local_step, mesh=mesh, in_specs=placed, out_specs=P(("attn", "exp"), "tp"), check_vma=False
    )
```

time: 290 us -> 74.1 us (0.26)
  waiting for transfers between devices: 199 us -> 0 us
  Pallas kernels: 0 us -> 72.4 us
  matrix products: 28.3 us -> 0 us
  blocking collectives: 17.4 us -> 0 us
  other arithmetic: 14.3 us -> 0 us
  between operations: 13.3 us -> 0.01 us
  local copies, waits for them, and re-layouts: 11 us -> 1.52 us
  starting transfers between devices: 4.23 us -> 0 us
    reduce_scatter x1 -> x0, waiting for transfers between devices: 107 us -> none  [local(): lax.psum_scatter(term_rows, ('attn', 'tp'), scatter_dimension=0, tiled=True)]
    pallas_call x0 -> x1, Pallas kernels: none -> 72.4 us  [local_step(): pl.pallas_call(kernel, out_shape=jax.ShapeDtypeStruct((R, QD), BF16), in_...]
    psum x1 -> x0, waiting for transfers between devices: 44.8 us -> none  [local(): summed = lax.psum(partial_value, 'tp')]
    all_gather x1 -> x0, waiting for transfers between devices: 41.6 us -> none  [local(): lax.all_gather(incoming.reshape(1, slot_count * CAP, incoming.shape[2]),...]
    dot_general x9 -> x0, matrix products: 28.3 us -> none  [the longest x1 7.12 us: expert_rows(): result = jnp.dot(active, w_down[0], preferred_element_type=jnp.float32)]
    all_to_all x1 -> x0, blocking collectives: 17.4 us -> none  [local(): lax.all_to_all(outgoing, 'exp', split_axis=0, concat_axis=0, tiled=True)]
    convert_element_type x2 -> x0, other arithmetic: 6.54 us -> none  [the longest x1 5.5 us: expert_rows(): (flat_rows * lax.rsqrt(spread + 1e-05) * moe_gain[None, :]).astype(jnp.bf...]
    all_to_all x1 -> x0, waiting for transfers between devices: 5.62 us -> none  [local(): lax.all_to_all(answered, 'exp', split_axis=0, concat_axis=0, tiled=True)]
  transfers between devices with their start and end apart: 4 -> 0, of which waited for: 4 -> 0; matrix products, arithmetic and copies ran while one was open for 2% -> 0% of each run, Pallas kernels for 0% -> 0%
where the time goes in v3:
time: 74.1 us; the launch traced here: 73.9 us
  Pallas kernels  72.4 us (98%)
  local copies, waits for them, and re-layouts  1.52 us (2%)
    pallas_call x1, Pallas kernels, local_step(): pl.pallas_call(kernel, out_shape=jax.ShapeDtypeStruct((R, QD), BF16), in_...  72.4 us
    unnamed x1, local copies, waits for them, and re-layouts  1.52 us

profile of v3, /device:TPU:1, one launch (start us, length us, event | category | flops | bytes accessed | tf_op | source)
XLA Modules:
  0.0 73.9 jit_solution(3784991353684866028)
XLA Ops:
  0.0 72.4 %decode_layer.1 = bf16[24,1536]{1,0:T(8,128)(2,1)} custom-call(s32[24]{0:T(128)} %refs_0_.1, s32[4]{0:T(128)} %refs_1_.1, bf16[24,768]{1,0:T(8,128)(2,1)} %refs_2_.1, bf16[24,2,128]{2,1,0:T(2,128)(2,1)} %refs_3_.1, bf16[24,6144]{1,0:T(8,128)(2,1)} %refs_4_.1, s32[2,24]{1,0:T(2,128)} %bitcast.4, f32[2,24]{1,0:T(2,128)} %bitcast.5, f32[24,1,256]{2,1,0:T(1,128)} %bitcast.3, ...), custom_call_target="tpu_custom_call" | custom-call | tf_op jit(solution)/shard_map/decode_layer/pallas_call | solution.py:590
  72.4 1.5 %copy.15 = bf16[24,1536]{1,0:T(8,128)(2,1)} copy(bf16[24,1536]{1,0:T(8,128)(2,1)} %decode_layer.1) | data formatting | bytes 147456

commit v4 on v3

--- a/solution.py
+++ b/solution.py
@@ -49,6 +49,7 @@
         res_send=v((R, 3 * W), F32),
         res_recv=v((R, 3 * W), F32),
         hidden=v((2, R, 3 * W), F32),
+        hidden_in=v((R, 3 * W), F32),
         result=v((R, QD), F32),
         send_sems=pltpu.SemaphoreType.DMA((SENDS,)),
         recv_sems=pltpu.SemaphoreType.DMA((SEMS,)),
@@ -74,8 +75,8 @@
         row_out=v((3, 3, 4, b, W), BF16),
         row_in=v((3, 3, 4, b, W), BF16),
         row_own=v((3, 4, b, W), F32),
-        blk_out=v((3, 3, b, W), BF16),
-        blk_in=v((3, 3, b, W), BF16),
+        blk_out=v((3, 3, 2, b, 128), BF16),
+        blk_in=v((3, 3, 2, b, 128), BF16),
         fin_send=v((2, 3, n, W), F32),
         fin=v((3, n, W), F32),
     )
@@ -94,6 +95,7 @@
     k_buf, v_buf, op_buf, wg, wu, wd = (m[k] for k in ("k_buf", "v_buf", "op_buf", "wg", "wu", "wd"))
     q_pad, kn, vn, scores, attn_out = (m[k] for k in ("q_pad", "kn", "vn", "scores", "attn_out"))
     info, res_send, res_recv, hidden, result = (m[k] for k in ("info", "res_send", "res_recv", "hidden", "result"))
+    hidden_in = m["hidden_in"]
     info_pad, send_sems, recv_sems, local_sems = (m[k] for k in ("info_pad", "send_sems", "recv_sems", "local_sems"))
 
     attn = lax.axis_index("attn")
@@ -138,7 +140,7 @@
 
     barrier = pltpu.get_barrier_semaphore()
     partners = [device(c=k, z=j) for j in (1, 2, 3) for k in (0, 1)] + [sibling]
-    partners += [device(**{a: j}) for a in ("x", "y") for j in (1, 2, 3)]
+    partners += [device(c=k, **{a: j}) for a in ("x", "y") for j in (1, 2, 3) for k in (0, 1)]
     for p in partners:
         pl.semaphore_signal(barrier, inc=1, device_id=p, device_id_type=MESH)
 
@@ -296,7 +298,7 @@
         def pass_on(s, j):
             p1, p2, p3 = place[s]
             spot = x_all.at[c, s, p3, p2, wrap(p1 - j)]
-            for k in (2, 1, 3):
+            for k in (1, 3, 2):
                 send(spot, spot, ("g2", t), ("g2", t, k), device(**{STREAMS[s][1]: k}))
             for k in (1, 3):
                 send(spot, spot, ("g3", t), ("g3", t, 0), device(**{STREAMS[s][2]: k}))
@@ -323,6 +325,7 @@
                 send(spot, spot, ("g1", t), ("g1", t, j), device(**{a1: j}))
         for s in range(3):
             pass_on(s, 0)
+        send(hidden.at[other], hidden_in, "hid", "hid", sibling)
 
         def row(s, j3, j2, core):
             _, p2, p3 = place[s]
@@ -533,15 +536,28 @@
                     send(row_out.at[s, j2 - 1], row_in.at[s, j2 - 1], ("r2", t), ("r2", t, s), to)
                 else:
                     row_own[s] = v
+        def fold(v):
+            return jnp.concatenate([v[:, :128], v[:, 128:]], axis=0).astype(BF16)
+
+        def unfold(v):
+            v = v.astype(F32)
+            return jnp.concatenate([v[:n], v[n:]], axis=1)
+
         for s in range(3):
             arrived(row_in.at[s], ("r2", t, s))
             row_own[s] = row_own[s] + (
                 row_in[s, 0].astype(F32) + row_in[s, 1].astype(F32) + row_in[s, 2].astype(F32)
             )
             for j1 in (2, 1, 3):
-                blk_out[s, j1 - 1] = row_own[s, wrap(place[s][0] + j1)].astype(BF16)
-                to = device(**{STREAMS[s][0]: j1})
-                send(blk_out.at[s, j1 - 1], blk_in.at[s, j1 - 1], ("r1", t), ("r1", t, s), to)
+                v = row_own[s, wrap(place[s][0] + j1)]
+                for k in range(2):
+                    blk_out[s, j1 - 1, k] = fold(v[k * n : (k + 1) * n])
+                    to = device(c=k, **{STREAMS[s][0]: j1})
+                    send(blk_out.at[s, j1 - 1, k], blk_in.at[s, j1 - 1, c], ("r1", t), ("r1", t, s), to)
+            v = row_own[s, place[s][0]]
+            for k in range(2):
+                fin_send[k, s] = v[k * n : (k + 1) * n]
+            send(fin_send.at[other, s], fin.at[s], ("fin", t), ("fin", t), sibling)
         drain(z_send, ("z", t))
         drain(z_sib.at[0], ("zs", t))
         drain(x_all.at[c, :, 0, 0, pl.ds(0, 3)], ("g1", t))
@@ -552,21 +568,23 @@
         drain(d2_in, ("r4", t))
         drain(plane_in, ("r3", t))
         drain(row_out, ("r2", t))
-        for s in range(3):
-            v = row_own[s, place[s][0]]
+        drain(hidden_in, "hid")
+        arrived(hidden_in, "hid")
+        arrived(fin, ("fin", t))
+        drain(fin, ("fin", t))
+        for s in range(3):
+            cols = slice(s * W, (s + 1) * W)
+            mine = hidden[c, :, cols] + fin_send[c, s]
+            theirs = hidden_in[:, cols] + fin[s]
             arrived(blk_in.at[s], ("r1", t, s))
             for j in range(3):
-                v = v + blk_in[s, j].astype(F32)
-            for k in range(2):
-                fin_send[k, s] = hidden[k, rows, s * W : (s + 1) * W] + v[k * n : (k + 1) * n]
-            send(fin_send.at[other, s], fin.at[s], ("fin", t), ("fin", t), sibling)
-        drain(blk_out, ("r1", t))
-        arrived(fin, ("fin", t))
-        drain(fin, ("fin", t))
-        for s in range(3):
-            fin_send[other, s] = fin[s]
+                mine = mine + unfold(blk_in[s, j, c])
+                theirs = theirs + unfold(blk_in[s, j, other])
+            fin_send[c, s] = mine
+            fin_send[other, s] = theirs
             for h in range(2):
                 result[rows, s * 512 + h * W : s * 512 + (h + 1) * W] = fin_send[h, s]
+        drain(blk_out, ("r1", t))
 
     flow(0)
     drain(res_send, "res")

time: 74.1 us -> 72.2 us (0.974)
  Pallas kernels: 72.4 us -> 70.5 us
    pallas_call x1, Pallas kernels: 72.4 us -> 70.5 us  [local_step(): pl.pallas_call(kernel, out_shape=jax.ShapeDtypeStruct((R, QD), BF16), in_...]
where the time goes in v4:
time: 72.2 us; the launch traced here: 72.1 us
  Pallas kernels  70.5 us (98%)
  local copies, waits for them, and re-layouts  1.52 us (2%)
    pallas_call x1, Pallas kernels, local_step(): pl.pallas_call(kernel, out_shape=jax.ShapeDtypeStruct((R, QD), BF16), in_...  70.5 us
    unnamed x1, local copies, waits for them, and re-layouts  1.52 us

profile of v4, /device:TPU:1, one launch (start us, length us, event | category | flops | bytes accessed | tf_op | source)
XLA Modules:
  0.0 72.1 jit_solution(3219454132774675870)
XLA Ops:
  0.0 70.5 %decode_layer.1 = bf16[24,1536]{1,0:T(8,128)(2,1)} custom-call(s32[24]{0:T(128)} %refs_0_.1, s32[4]{0:T(128)} %refs_1_.1, bf16[24,768]{1,0:T(8,128)(2,1)} %refs_2_.1, bf16[24,2,128]{2,1,0:T(2,128)(2,1)} %refs_3_.1, bf16[24,6144]{1,0:T(8,128)(2,1)} %refs_4_.1, s32[2,24]{1,0:T(2,128)} %bitcast.4, f32[2,24]{1,0:T(2,128)} %bitcast.5, f32[24,1,256]{2,1,0:T(1,128)} %bitcast.3, ...), custom_call_target="tpu_custom_call" | custom-call | tf_op jit(solution)/shard_map/decode_layer/pallas_call | solution.py:608
  70.5 1.5 %copy.15 = bf16[24,1536]{1,0:T(8,128)(2,1)} copy(bf16[24,1536]{1,0:T(8,128)(2,1)} %decode_layer.1) | data formatting | bytes 147456

commit v5 on v4

--- a/solution.py
+++ b/solution.py
@@ -16,7 +16,7 @@
 D = 6144
 QD = 1536
 W = 256
-SEMS = 44
+SEMS = 46
 SENDS = 20
 PARTS = ((0, R),)
 CHUNK = 6
@@ -320,7 +320,7 @@
         for s, (a1, a2, a3) in enumerate(STREAMS):
             p1, p2, p3 = place[s]
             x_all[c, s, p3, p2, p1] = sent[:, s * W : (s + 1) * W]
-            for j in (2, 1, 3):
+            for j in (1, 3, 2):
                 spot = x_all.at[c, s, p3, p2, p1]
                 send(spot, spot, ("g1", t), ("g1", t, j), device(**{a1: j}))
         for s in range(3):
@@ -419,17 +419,15 @@
         if t == 0:
             for cp in w_copies:
                 cp.wait()
-        shared(0, 0)
-        rows_01((0,), (0,))
         take2(1)
         take2(3)
         take2(2)
         take3(0)
         info_2()
+        shared(0, 0)
         shared(0, 1)
-        rows_01((0,), (1, 3))
+        rows_01((0,), (0, 1, 3, 2))
         take3(1)
-        rows_01((0,), (2,))
         planes_2((0,))
         take3(3)
         shared(1, 0)
@@ -453,21 +451,26 @@
             arrived(info.at[other], "ic")
         lane4 = lax.broadcasted_iota(jnp.int32, (4, b, 128), 2)
 
-        def activate(i, carry):
+        def activate(step, carry):
+            i = wrap(me["y"] + 2 + step)
             both = jnp.concatenate([info[0, i, :, rows], info[1, i, :, rows]], axis=1)
             chosen = jnp.sum(jnp.where(lane4 == me["x"], both, 0.0), axis=2, keepdims=True)
             inv = lax.rsqrt(jnp.sum(ssum[i], axis=2, keepdims=True) / D + 1e-05)
             g = acc_g[i] * inv
             u = acc_u[i] * inv
             act[c, i] = (g / (1.0 + jnp.exp(-g)) * u * chosen).astype(BF16)
-            send(act.at[c, i], act.at[c, i], ("act", t), ("act", t), sibling)
+            send(act.at[c, i], act.at[c, i], ("act", t), key, sibling)
             return carry
 
-        lax.fori_loop(0, 4, activate, 0, unroll=2)
+        key = ("act", t, 0)
+        activate(0, 0)
+        key = ("act", t, 1)
+        for step in (1, 2, 3):
+            activate(step, 0)
         if t == 0:
             local(wd.at[:, :, down_rows(0)], wd.at[:, :, down_rows(0)], 6).wait()
             arrived(wd.at[:, :, down_rows(0)], "wd")
-        arrived(act.at[other], ("act", t))
+        arrived(act.at[other, 0], ("act", t, 0))
 
         def down(s, j3):
             q = wrap(place[s][2] + j3)
@@ -507,7 +510,10 @@
                 part[s, j, r] = (part[s, j, r].astype(F32) + d2_in[s, r].astype(F32)).astype(BF16)
                 send_near(s, j, j2)
 
-        for s in range(3):
+        down(2, 2)
+        send_far(2)
+        arrived(act.at[other, pl.ds(0, 3)], ("act", t, 1))
+        for s in range(2):
             down(s, 2)
             send_far(s)
         for s in range(3):

time: 72.2 us -> 70.8 us (0.981)
  Pallas kernels: 70.5 us -> 69.1 us
    pallas_call x1, Pallas kernels: 70.5 us -> 69.1 us  [local_step(): pl.pallas_call(kernel, out_shape=jax.ShapeDtypeStruct((R, QD), BF16), in_...]
where the time goes in v5:
time: 70.8 us; the launch traced here: 70.6 us
  Pallas kernels  69.1 us (98%)
  local copies, waits for them, and re-layouts  1.52 us (2%)
    pallas_call x1, Pallas kernels, local_step(): pl.pallas_call(kernel, out_shape=jax.ShapeDtypeStruct((R, QD), BF16), in_...  69.1 us
    unnamed x1, local copies, waits for them, and re-layouts  1.52 us

profile of v5, /device:TPU:1, one launch (start us, length us, event | category | flops | bytes accessed | tf_op | source)
XLA Modules:
  0.0 70.6 jit_solution(4392610922140727109)
XLA Ops:
  0.0 69.1 %decode_layer.1 = bf16[24,1536]{1,0:T(8,128)(2,1)} custom-call(s32[24]{0:T(128)} %refs_0_.1, s32[4]{0:T(128)} %refs_1_.1, bf16[24,768]{1,0:T(8,128)(2,1)} %refs_2_.1, bf16[24,2,128]{2,1,0:T(2,128)(2,1)} %refs_3_.1, bf16[24,6144]{1,0:T(8,128)(2,1)} %refs_4_.1, s32[2,24]{1,0:T(2,128)} %bitcast.4, f32[2,24]{1,0:T(2,128)} %bitcast.5, f32[24,1,256]{2,1,0:T(1,128)} %bitcast.3, ...), custom_call_target="tpu_custom_call" | custom-call | tf_op jit(solution)/shard_map/decode_layer/pallas_call | solution.py:614
  69.1 1.5 %copy.15 = bf16[24,1536]{1,0:T(8,128)(2,1)} copy(bf16[24,1536]{1,0:T(8,128)(2,1)} %decode_layer.1) | data formatting | bytes 147456

commit v6 on v5

--- a/solution.py
+++ b/solution.py
@@ -472,7 +472,7 @@
             arrived(wd.at[:, :, down_rows(0)], "wd")
         arrived(act.at[other, 0], ("act", t, 0))
 
-        def down(s, j3):
+        def down(s, j3, steps=None):
             q = wrap(place[s][2] + j3)
 
             def step(i, carry):
@@ -486,13 +486,17 @@
                     part[s, j3, i] = y
                 return carry
 
-            lax.fori_loop(0, 4, step, 0, unroll=4)
+            if steps is None:
+                lax.fori_loop(0, 4, step, 0, unroll=4)
+            else:
+                for i in steps:
+                    step(i, 0)
 
         def second(s, j2):
             return wrap(place[s][1] + j2)
 
-        def send_far(s):
-            for j2 in (2, 3, 1, 0):
+        def send_far(s, rows=(2, 3, 1, 0)):
+            for j2 in rows:
                 j = 1 if j2 in FORWARD_UP else 3
                 r = second(s, j2)
                 send(part.at[s, 2, r], d2_in.at[s, r], ("r4", t), ("r4", t, j2), device(**{STREAMS[s][2]: j}))
@@ -512,10 +516,13 @@
 
         down(2, 2)
         send_far(2)
+        down(0, 2, [second(0, 2)])
+        send_far(0, (2,))
         arrived(act.at[other, pl.ds(0, 3)], ("act", t, 1))
-        for s in range(2):
-            down(s, 2)
-            send_far(s)
+        down(0, 2, [second(0, j2) for j2 in (3, 1, 0)])
+        send_far(0, (3, 1, 0))
+        down(1, 2)
+        send_far(1)
         for s in range(3):
             down(s, 1)
             send_near(s, 1, 2)

time: 70.8 us -> 70.9 us (level)
  no operation moved by 1% of the time
where the time goes in v6:
time: 70.9 us; the launch traced here: 70.8 us
  Pallas kernels  69.2 us (98%)
  local copies, waits for them, and re-layouts  1.52 us (2%)
    pallas_call x1, Pallas kernels, local_step(): pl.pallas_call(kernel, out_shape=jax.ShapeDtypeStruct((R, QD), BF16), in_...  69.2 us
    unnamed x1, local copies, waits for them, and re-layouts  1.52 us

profile of v6, /device:TPU:1, one launch (start us, length us, event | category | flops | bytes accessed | tf_op | source)
XLA Modules:
  0.0 70.8 jit_solution(4226249550522399403)
XLA Ops:
  0.0 69.2 %decode_layer.1 = bf16[24,1536]{1,0:T(8,128)(2,1)} custom-call(s32[24]{0:T(128)} %refs_0_.1, s32[4]{0:T(128)} %refs_1_.1, bf16[24,768]{1,0:T(8,128)(2,1)} %refs_2_.1, bf16[24,2,128]{2,1,0:T(2,128)(2,1)} %refs_3_.1, bf16[24,6144]{1,0:T(8,128)(2,1)} %refs_4_.1, s32[2,24]{1,0:T(2,128)} %bitcast.4, f32[2,24]{1,0:T(2,128)} %bitcast.5, f32[24,1,256]{2,1,0:T(1,128)} %bitcast.3, ...), custom_call_target="tpu_custom_call" | custom-call | tf_op jit(solution)/shard_map/decode_layer/pallas_call | solution.py:621
  69.2 1.5 %copy.15 = bf16[24,1536]{1,0:T(8,128)(2,1)} copy(bf16[24,1536]{1,0:T(8,128)(2,1)} %decode_layer.1) | data formatting | bytes 147456
